TPU v7x, 32 devices: a whole 2x2x4 slice. The times are simulated.
32 devices in a mesh: dp: 4 (over y, core), expert: 8 (over z, x).
Axes of the slice: x: 2, y: 2, z: 4, core: 2. Of those that a mesh axis runs over, the one named last changes fastest.
Arguments:
- tokens: bfloat16 [2, 8192, 768], P(None, ('dp', 'expert')), may hold values from -6 to 6
- gain_attn: float32 [768], replicated, may hold values from 0.25 to 1.75
- qkv_weight: bfloat16 [768, 2304], P(('dp', 'expert')), may hold values from -0.21875 to 0.21875
- out_weight: bfloat16 [768, 768], P(('dp', 'expert')), may hold values from -1.25 to 1.25
- bias_table: float32 [32, 12], replicated, may hold values from -4 to 4
- gain_ffn: float32 [768], replicated, may hold values from 0.25 to 1.75
- router_weight: bfloat16 [768, 16], P(('dp', 'expert')), may hold values from -0.14941406 to 0.14941406
- expert_in: bfloat16 [16, 768, 3072], P('expert', None, 'dp'), may hold values from -0.21875 to 0.21875
- expert_out: bfloat16 [16, 3072, 768], P('expert', 'dp'), may hold values from -0.15625 to 0.15625
- lengths: int32 [2, 32, 4], P(None, ('dp', 'expert')), may hold values from 1 to 160, 256 in all within a row
- buckets: int32 [256], replicated, may hold values from 0 to 31, as said below
- routes: int32 [2, 8192, 2], P(None, ('dp', 'expert')), may hold values from 0 to 15, all different within a row; in each aligned block of 256 rows (0 to 255, 256 to 511, ..., all dimensions but the last counted through in order) at most 48 rows name the same one
- cotangent: bfloat16 [2, 8192, 768], P(None, ('dp', 'expert')), may hold values from -6 to 6
Outputs:
- block_out: bfloat16 [2, 8192, 768], P(None, ('dp', 'expert'))
- tokens_grad: bfloat16 [2, 8192, 768], P(None, ('dp', 'expert'))
- gain_attn_grad: float32 [768], replicated
- qkv_grad: float32 [768, 2304], P(('dp', 'expert'))
- out_grad: float32 [768, 768], P(('dp', 'expert'))
- table_grad: float32 [32, 12], replicated
- gain_ffn_grad: float32 [768], replicated
- router_grad: float32 [768, 16], P(('dp', 'expert'))
- expert_in_grad: float32 [16, 768, 3072], P('expert', None, 'dp')
- expert_out_grad: float32 [16, 3072, 768], P('expert', 'dp')
Inputs may be any that keep to these rules, and one draw needn't show every extreme that they name: The 4 lengths of each device's micro-batch sum to 256. `buckets`: Non-decreasing in the distance, 0 at distance 0 and 31 at the largest distance. `routes`: A token's two experts differ; in each micro-batch the 256 tokens of one device name one expert at most 48 times.
All inputs are finite; a program needn't handle non-finite values.
Results may differ from a plain program's by a relative error of at most 0.013.
Values may be sent and summed in bfloat16 or wider, within the bound.
A program may use at most 192 MiB of HBM per device.

v0:
```python
import jax
import jax.numpy as jnp
from jax import lax
from jax.sharding import PartitionSpec as P

EPSILON = 1e-06
HIGHEST = lax.Precision.HIGHEST


def rms_norm(values, gain_vec):
    return (
        values * lax.rsqrt(jnp.mean(values * values, axis=-1, keepdims=True) + EPSILON) * gain_vec
    )


def gelu_tanh(values):
    return jax.nn.gelu(values, approximate=True)


def attention_scores(queries, key_rows, bias_full, allowed, score_scale):
    scores = (
        jnp.einsum("mqhd,mkhd->mhqk", queries, key_rows, preferred_element_type=jnp.float32)
        * score_scale
        + bias_full[None]
    )
    return jnp.where(allowed[:, None], scores, -1e30)


def on_device(
    tokens,
    gain_attn,
    qkv_weight,
    out_weight,
    bias_table,
    gain_ffn,
    router_weight,
    expert_in,
    expert_out,
    lengths,
    buckets,
    routes,
    cotangent,
):
    micro, tok_mb, model_width = tokens.shape
    experts = router_weight.shape[1]
    capacity = 3 * tok_mb // experts
    bucket_count, head_count = bias_table.shape
    head_size = model_width // head_count
    score_scale = head_size ** (-0.5)
    row_count = micro * tok_mb
    pair_count = 2 * tok_mb
    qkv_full, out_full, router_full = (
        lax.all_gather(qkv_weight, ("dp", "expert"), axis=0, tiled=True),
        lax.all_gather(out_weight, ("dp", "expert"), axis=0, tiled=True),
        lax.all_gather(router_weight, ("dp", "expert"), axis=0, tiled=True),
    )
    in_full, back_full = (
        lax.all_gather(expert_in, "dp", axis=2, tiled=True),
        lax.all_gather(expert_out, "dp", axis=1, tiled=True),
    )
    flat_x = tokens.astype(jnp.float32).reshape(row_count, model_width)
    normed_low = rms_norm(flat_x, gain_attn).astype(jnp.bfloat16)
    qkv_act = jnp.dot(normed_low, qkv_full, preferred_element_type=jnp.float32).astype(jnp.bfloat16)
    queries = qkv_act[:, :model_width].reshape(micro, tok_mb, head_count, head_size)
    key_rows = qkv_act[:, model_width : 2 * model_width].reshape(
        micro, tok_mb, head_count, head_size
    )
    value_rows = qkv_act[:, 2 * model_width :].reshape(micro, tok_mb, head_count, head_size)
    positions = jnp.arange(tok_mb, dtype=jnp.int32)
    seq_ends = jnp.cumsum(lengths[:, 0, :], axis=1)
    segment = jnp.sum((positions[None, :, None] >= seq_ends[:, None, :]).astype(jnp.int32), axis=2)
    allowed = (positions[:, None] >= positions[None, :])[None] & (
        segment[:, :, None] == segment[:, None, :]
    )
    distance = jnp.maximum(positions[:, None] - positions[None, :], 0)
    bucket_ids = jnp.arange(bucket_count, dtype=jnp.int32)
    thresholds = jnp.sum((buckets[None, :] < bucket_ids[:, None]).astype(jnp.int32), axis=1)
    distance_bucket = jnp.sum(
        (distance[:, :, None] >= thresholds[1:][None, None, :]).astype(jnp.int32), axis=2
    )
    bucket_hot = (distance_bucket[:, :, None] == bucket_ids).astype(jnp.float32)
    bias_full = jnp.einsum("qkb,bh->hqk", bucket_hot, bias_table, precision=HIGHEST)
    scores = attention_scores(queries, key_rows, bias_full, allowed, score_scale)
    row_max = jnp.max(scores, axis=-1, keepdims=True)
    row_sum = jnp.sum(jnp.exp(scores - row_max), axis=-1, keepdims=True)
    log_total = row_max + jnp.log(row_sum)
    probability = jnp.exp(scores - log_total)
    context = jnp.einsum(
        "mhqk,mkhd->mqhd",
        probability.astype(jnp.bfloat16),
        value_rows,
        preferred_element_type=jnp.float32,
    )
    context = context.reshape(row_count, model_width).astype(jnp.bfloat16)
    middle = flat_x + jnp.dot(context, out_full, preferred_element_type=jnp.float32)
    ffn_low = rms_norm(middle, gain_ffn).astype(jnp.bfloat16)
    logits = jnp.dot(ffn_low, router_full, preferred_element_type=jnp.float32)
    expert_ids = jnp.arange(experts, dtype=jnp.int32)
    route_hot = (routes.reshape(row_count, 2)[:, :, None] == expert_ids).astype(jnp.float32)
    chosen = jnp.sum(route_hot * logits[:, None, :], axis=2)
    gate_weights = jax.nn.softmax(chosen, axis=-1)
    route_rows = routes.reshape(micro, pair_count)
    expert_hits = (route_rows[:, :, None] == expert_ids).astype(jnp.float32)
    pair_pos = jnp.arange(pair_count, dtype=jnp.int32)
    strict_lower = (pair_pos[None, :] < pair_pos[:, None]).astype(jnp.float32)
    earlier = jnp.einsum("ij,mje->mie", strict_lower, expert_hits, precision=HIGHEST)
    slot_rank = jnp.sum(earlier * expert_hits, axis=2)
    slot_ids = jnp.arange(capacity, dtype=jnp.float32)
    rank_hot = (slot_rank[:, :, None] == slot_ids).astype(jnp.float32)
    slot_hot = (expert_hits[:, :, :, None] * rank_hot[:, :, None, :]).reshape(
        micro, pair_count, experts * capacity
    )
    slot_hot = slot_hot.astype(jnp.bfloat16)
    copies = jnp.repeat(ffn_low, 2, axis=0).reshape(micro, pair_count, model_width)
    send_rows = jnp.einsum(
        "mns,mnd->msd", slot_hot, copies, preferred_element_type=jnp.float32
    ).astype(jnp.bfloat16)
    send_rows = send_rows.reshape(micro, experts, capacity, model_width)
    received = lax.all_to_all(send_rows, "expert", split_axis=1, concat_axis=2, tiled=True)
    pre_act = jnp.einsum("merd,edf->merf", received, in_full, preferred_element_type=jnp.float32)
    hidden = gelu_tanh(pre_act).astype(jnp.bfloat16)
    produced = jnp.einsum(
        "merf,efd->merd", hidden, back_full, preferred_element_type=jnp.float32
    ).astype(jnp.bfloat16)
    returned = lax.all_to_all(produced, "expert", split_axis=2, concat_axis=1, tiled=True)
    returned, received, pre_act, hidden = (returned, received, pre_act, hidden)
    returned_flat = returned.reshape(micro, experts * capacity, model_width)
    back_rows = jnp.einsum(
        "mns,msd->mnd", slot_hot, returned_flat, preferred_element_type=jnp.float32
    )
    back_rows = back_rows.reshape(row_count, 2, model_width)
    mixture = jnp.sum(gate_weights[:, :, None] * back_rows, axis=1)
    block_out = (middle + mixture).astype(jnp.bfloat16).reshape(tokens.shape)
    qkv_back, out_back, router_back = (
        lax.all_gather(qkv_weight, ("dp", "expert"), axis=0, tiled=True),
        lax.all_gather(out_weight, ("dp", "expert"), axis=0, tiled=True),
        lax.all_gather(router_weight, ("dp", "expert"), axis=0, tiled=True),
    )
    in_back, second_back = (
        lax.all_gather(expert_in, "dp", axis=2, tiled=True),
        lax.all_gather(expert_out, "dp", axis=1, tiled=True),
    )
    grad_out = cotangent.astype(jnp.float32).reshape(row_count, model_width)
    grad_gate = jnp.sum(grad_out[:, None, :] * back_rows, axis=2)
    grad_copy = (
        (gate_weights[:, :, None] * grad_out[:, None, :])
        .astype(jnp.bfloat16)
        .reshape(micro, pair_count, model_width)
    )
    grad_send = jnp.einsum(
        "mns,mnd->msd", slot_hot, grad_copy, preferred_element_type=jnp.float32
    ).astype(jnp.bfloat16)
    grad_send = grad_send.reshape(micro, experts, capacity, model_width)
    grad_recv = lax.all_to_all(grad_send, "expert", split_axis=1, concat_axis=2, tiled=True)
    grad_hidden = jnp.einsum(
        "merd,efd->merf", grad_recv, second_back, preferred_element_type=jnp.float32
    )
    grad_pre = jax.vjp(gelu_tanh, pre_act)[1](grad_hidden)[0].astype(jnp.bfloat16)
    grad_in_rows = jnp.einsum(
        "merf,edf->merd", grad_pre, in_back, preferred_element_type=jnp.float32
    ).astype(jnp.bfloat16)
    grad_back = lax.all_to_all(grad_in_rows, "expert", split_axis=2, concat_axis=1, tiled=True)
    grad_back_flat = grad_back.reshape(micro, experts * capacity, model_width)
    grad_pairs = jnp.einsum(
        "mns,msd->mnd", slot_hot, grad_back_flat, preferred_element_type=jnp.float32
    )
    grad_ffn = jnp.sum(grad_pairs.reshape(row_count, 2, model_width), axis=1)
    part_in = jnp.einsum("merd,merf->edf", received, grad_pre, preferred_element_type=jnp.float32)
    part_out = jnp.einsum("merf,merd->efd", hidden, grad_recv, preferred_element_type=jnp.float32)
    expert_in_grad, expert_out_grad = (
        lax.psum_scatter(
            part_in.astype(jnp.bfloat16), "dp", scatter_dimension=2, tiled=True
        ).astype(jnp.float32),
        lax.psum_scatter(
            part_out.astype(jnp.bfloat16), "dp", scatter_dimension=1, tiled=True
        ).astype(jnp.float32),
    )
    gate_mean = jnp.sum(gate_weights * grad_gate, axis=1, keepdims=True)
    grad_chosen = gate_weights * (grad_gate - gate_mean)
    grad_logits = jnp.sum(route_hot * grad_chosen[:, :, None], axis=1).astype(jnp.bfloat16)
    router_part = jnp.einsum("nd,ne->de", ffn_low, grad_logits, preferred_element_type=jnp.float32)
    grad_ffn = grad_ffn + jnp.einsum(
        "ne,de->nd", grad_logits, router_back, preferred_element_type=jnp.float32
    )
    grad_mid_part, gain_ffn_part = jax.vjp(rms_norm, middle, gain_ffn)[1](grad_ffn)
    grad_middle = grad_out + grad_mid_part
    grad_attn = grad_middle.astype(jnp.bfloat16)
    out_part = jnp.einsum("nc,nd->cd", context, grad_attn, preferred_element_type=jnp.float32)
    grad_context = jnp.einsum(
        "nd,cd->nc", grad_attn, out_back, preferred_element_type=jnp.float32
    ).astype(jnp.bfloat16)
    grad_context = grad_context.reshape(micro, tok_mb, head_count, head_size)
    scores_again = attention_scores(queries, key_rows, bias_full, allowed, score_scale)
    prob_again = jnp.exp(scores_again - log_total)
    grad_prob = jnp.einsum(
        "mqhd,mkhd->mhqk", grad_context, value_rows, preferred_element_type=jnp.float32
    )
    row_delta = jnp.sum(prob_again * grad_prob, axis=-1, keepdims=True)
    grad_scores = (prob_again * (grad_prob - row_delta)).astype(jnp.bfloat16)
    score_total = jnp.sum(grad_scores.astype(jnp.float32), axis=0)
    table_part = jnp.einsum("hqk,qkb->bh", score_total, bucket_hot, precision=HIGHEST)
    grad_queries = (
        jnp.einsum("mhqk,mkhd->mqhd", grad_scores, key_rows, preferred_element_type=jnp.float32)
        * score_scale
    )
    grad_keys = (
        jnp.einsum("mhqk,mqhd->mkhd", grad_scores, queries, preferred_element_type=jnp.float32)
        * score_scale
    )
    grad_values = jnp.einsum(
        "mhqk,mqhd->mkhd",
        prob_again.astype(jnp.bfloat16),
        grad_context,
        preferred_element_type=jnp.float32,
    )
    grad_qkv = jnp.concatenate(
        [
            grad_queries.reshape(row_count, model_width),
            grad_keys.reshape(row_count, model_width),
            grad_values.reshape(row_count, model_width),
        ],
        axis=1,
    ).astype(jnp.bfloat16)
    qkv_part = jnp.einsum("nc,nd->cd", normed_low, grad_qkv, preferred_element_type=jnp.float32)
    grad_normed = jnp.einsum("nd,cd->nc", grad_qkv, qkv_back, preferred_element_type=jnp.float32)
    grad_x_part, gain_attn_part = jax.vjp(rms_norm, flat_x, gain_attn)[1](grad_normed)
    tokens_grad = (grad_middle + grad_x_part).astype(jnp.bfloat16).reshape(tokens.shape)
    qkv_grad, out_grad, router_grad = (
        lax.psum_scatter(qkv_part, ("dp", "expert"), scatter_dimension=0, tiled=True),
        lax.psum_scatter(out_part, ("dp", "expert"), scatter_dimension=0, tiled=True),
        lax.psum_scatter(router_part, ("dp", "expert"), scatter_dimension=0, tiled=True),
    )
    gain_attn_grad, table_grad, gain_ffn_grad = lax.psum(
        (gain_attn_part, table_part, gain_ffn_part), ("dp", "expert")
    )
    return (
        block_out,
        tokens_grad,
        gain_attn_grad,
        qkv_grad,
        out_grad,
        table_grad,
        gain_ffn_grad,
        router_grad,
        expert_in_grad,
        expert_out_grad,
    )


def solution(mesh):
    return jax.shard_map(
        on_device,
        mesh=mesh,
        in_specs=(
            P(None, ("dp", "expert"), None),
            P(),
            P(("dp", "expert"), None),
            P(("dp", "expert"), None),
            P(),
            P(),
            P(("dp", "expert"), None),
            P("expert", None, "dp"),
            P("expert", "dp", None),
            P(None, ("dp", "expert"), None),
            P(),
            P(None, ("dp", "expert"), None),
            P(None, ("dp", "expert"), None),
        ),
        out_specs=(
            P(None, ("dp", "expert"), None),
            P(None, ("dp", "expert"), None),
            P(),
            P(("dp", "expert"), None),
            P(("dp", "expert"), None),
            P(),
            P(),
            P(("dp", "expert"), None),
            P("expert", None, "dp"),
            P("expert", "dp", None),
        ),
        check_vma=False,
    )
```

profile of v0, /device:TPU:0, one launch (start us, length us, event | category | flops | bytes accessed | tf_op | source)
XLA Modules:
  0.0 811.5 jit_solution(12291724932084931981)
XLA Ops:
  13.4 11.6 %copy.126 = pred[256,256,32]{1,2,0:T(32,128)(4,1)S(1)} copy(pred[256,256,32]{0,2,1:T(32,128)(4,1)S(1)} %iota_compare_fusion) | data formatting | bytes 4194304 | tf_op jit(solution)/shard_map/eq | solution.py:81
  36.5 37.4 %all-gather.6.cloned.1.call-done = bf16[768,2304]{1,0:T(8,128)(2,1)} async-done(((bf16[24,2304]{1,0:T(8,128)(2,1)}), bf16[768,2304]{1,0:T(8,128)(2,1)}) %all-gather.6.cloned.1.call-update) | async-done | bytes 3538960 | tf_op jit(solution)/shard_map/all_gather | solution.py:53
  74.0 4.2 convolution_convert_fusion
  103.5 26.4 %all-gather.8.cloned.1.call-done = bf16[768,768]{1,0:T(8,128)(2,1)} async-done(((bf16[24,768]{1,0:T(8,128)(2,1)}), bf16[768,768]{1,0:T(8,128)(2,1)}) %all-gather.8.cloned.1.call-update) | async-done | bytes 1179664 | tf_op jit(solution)/shard_map/all_gather | solution.py:54
  141.3 4.6 all-to-all-start
  145.9 111.6 %all-gather = bf16[32,24,16]{1,2,0:T(8,128)(2,1)S(1)} all-gather(bf16[1,24,16]{1,2,0:T(8,128)(2,1)S(1)} %bitcast.224), channel_id=1, replica_groups=mesh['dp'=4,'expert'=8] {'dp','expert'}, dimensions={0}, use_global_device_ids=true | all-gather | bytes 25344 | tf_op jit(solution)/shard_map/all_gather | solution.py:55
  275.0 4.4 all-to-all-start.2
  282.7 47.7 %all-to-all-done.2 = bf16[2,16,48,768]{3,2,0,1:T(8,128)(2,1)} async-done(((bf16[2,16,48,768]{3,2,0,1:T(8,128)(2,1)}), bf16[2,16,48,768]{3,2,0,1:T(8,128)(2,1)}, u32[]{:S(2)}, u32[]{:S(2)}) %all-to-all-start.2) | async-done | bytes 2359328 | tf_op jit(solution)/shard_map/all_to_all | solution.py:154
  333.7 15.6 %fusion.13 = f32[2,2,384,3072]{3,2,1,0:T(8,128)} fusion(bf16[2,2,384,768]{3,2,0,1:T(8,128)(2,1)} %bitcast.212, bf16[2,768,3072]{2,1,0:T(8,128)(2,1)} %all-gather.10.cloned.1.call-done), kind=kOutput, calls=%fused_computation.20 | convolution fusion | flops 7247757312 | bytes 30670848 | tf_op jit(solution)/shard_map/merd,edf->merf/dot_general | solution.py:120
  349.3 16.9 %bitcast_convert_fusion = bf16[2,3072,768]{2,1,0:T(8,128)(2,1)} fusion(bf16[2,2,384,768]{3,2,0,1:T(8,128)(2,1)S(1)} %bitcast.215, f32[2,2,384,3072]{3,2,1,0:T(8,128)} %fusion.13), kind=kOutput, calls=%fused_computation.9 | convolution fusion | flops 7294943232 | bytes 30670848 | tf_op jit(solution)/shard_map/merf,merd->efd/dot_general | solution.py:169
  366.7 24.2 %fusion.6 = bf16[2,2,384,3072]{3,2,0,1:T(8,128)(2,1)} fusion(f32[2,2,384,3072]{3,2,1,0:T(8,128)} %fusion.13, bf16[2,2,384,768]{3,2,0,1:T(8,128)(2,1)} %bitcast.214, bf16[2,3072,768]{2,1,0:T(8,128)(2,1)} %all-gather.12.cloned.1.call-done), kind=kOutput, calls=%fused_computation.8 | convolution fusion | flops 7342129152 | bytes 40108032 | tf_op jit(solution)/shard_map/merd,efd->merf/dot_general | solution.py:155
  390.9 13.5 %bitcast_convert_fusion.1 = bf16[2,768,3072]{2,1,0:T(8,128)(2,1)} fusion(bf16[2,2,384,768]{3,2,0,1:T(8,128)(2,1)S(1)} %bitcast.213, bf16[2,2,384,3072]{3,2,0,1:T(8,128)(2,1)} %fusion.6), kind=kOutput, calls=%fused_computation.10 | convolution fusion | flops 7252475904 | bytes 21233664 | tf_op jit(solution)/shard_map/merd,merf->edf/dot_general | solution.py:168
  404.4 15.5 %convert_bitcast_fusion.1 = bf16[2,2,384,768]{3,2,0,1:T(8,128)(2,1)S(1)} fusion(bf16[2,3072,768]{2,1,0:T(8,128)(2,1)} %all-gather.12.cloned.1.call-done, f32[2,2,384,3072]{3,2,1,0:T(8,128)} %fusion.13), kind=kOutput, calls=%fused_computation.45 | convolution fusion | flops 7291404288 | bytes 30670848 | tf_op jit(solution)/shard_map/merf,efd->merd/dot_general | solution.py:122
  423.7 4.4 all-to-all-start.1
  428.1 13.0 %convert_bitcast_fusion = bf16[2,2,384,768]{3,2,0,1:T(8,128)(2,1)S(1)} fusion(bf16[2,2,384,3072]{3,2,0,1:T(8,128)(2,1)} %fusion.6, bf16[2,768,3072]{2,1,0:T(8,128)(2,1)} %all-gather.10.cloned.1.call-done), kind=kOutput, calls=%fused_computation.44 | convolution fusion | flops 7248936960 | bytes 21233664 | tf_op jit(solution)/shard_map/merf,edf->merd/dot_general | solution.py:159
  444.9 36.9 %all-to-all-done.1 = bf16[2,2,384,768]{3,0,1,2:T(2,128)(2,1)} async-done(((bf16[2,2,384,768]{3,0,1,2:T(2,128)(2,1)}), bf16[2,2,384,768]{3,0,1,2:T(2,128)(2,1)}, u32[]{:S(2)}, u32[]{:S(2)}) %all-to-all-start.1) | async-done | bytes 2359328 | tf_op jit(solution)/shard_map/all_to_all | solution.py:125
  481.8 4.4 all-to-all-start.3
  492.4 5.4 reshape.297
  497.8 41.8 %all-to-all-done.3 = bf16[2,2,384,768]{3,0,1,2:T(2,128)(2,1)} async-done(((bf16[2,2,384,768]{3,0,1,2:T(2,128)(2,1)}), bf16[2,2,384,768]{3,0,1,2:T(2,128)(2,1)}, u32[]{:S(2)}, u32[]{:S(2)}) %all-to-all-start.3) | async-done | bytes 2359328 | tf_op jit(solution)/shard_map/all_to_all | solution.py:162
  544.8 5.1 reshape.303
  550.0 5.7 reduce_sum.219
  557.6 15.3 %multiply_reduce_fusion.2 = f32[512,768]{1,0:T(8,128)S(1)} fusion(f32[512,2,768]{2,1,0:T(2,128)S(1)} %copy-done.11, f32[512,2]{1,0:T(8,128)S(1)} %copy.132), kind=kLoop, calls=%fused_computation.40 | loop fusion | flops 1179648 | bytes 4722688 | tf_op jit(solution)/shard_map/reduce_sum | solution.py:132
  586.4 7.4 multiply_reduce_fusion
  593.8 6.7 convert_reduce_fusion.1
  605.7 4.9 fusion.80
  612.9 5.5 fusion.44
  618.4 5.6 fusion.34
  624.0 39.1 %all-reduce.1 = (f32[768]{0:T(1024)}, f32[32,12]{0,1:T(8,128)}, f32[768]{0:T(1024)}, f32[768,16]{0,1:T(8,128)S(1)}) all-reduce(f32[768]{0:T(1024)S(1)} %get-tuple-element.12, f32[32,12]{0,1:T(8,128)S(1)} %fusion.44, f32[768]{0:T(1024)S(1)} %get-tuple-element.10, ...), channel_id=1, replica_groups=mesh['dp'=4,'expert'=8] {'dp','expert'}, use_global_device_ids=true, to_apply=%region_21.22 | all-reduce | flops 14208 | bytes 113664 | tf_op jit(solution)/shard_map/psum | solution.py:233
  666.5 4.2 convert_element_type.154
  670.7 4.2 convert_element_type.152
  675.0 4.3 reduce-scatter.8.cloned.1.call-done
  679.2 125.2 %reduce-scatter.6.cloned.1.call-done = f32[24,2304]{1,0:T(8,128)} async-done(((f32[768,2304]{1,0:T(8,128)}), f32[24,2304]{1,0:T(8,128)}) %reduce-scatter.6.cloned.1.call-update) | async-done | bytes 221200 | tf_op jit(solution)/shard_map/reduce_scatter | solution.py:229
  (232 shorter events, 123.6 us)
Async XLA Ops:
  7.2 17.9 %copy-start = (f32[32,12]{0,1:T(8,128)S(1)}, f32[32,12]{0,1:T(8,128)}, u32[]{:S(2)}) copy-start(f32[32,12]{0,1:T(8,128)} %param.17) | copy-start | bytes 4612
  7.2 66.7 %all-gather.6.cloned.1.call-start = ((), (), s32[]{:S(2)}) async-start(), calls=%async_computation.8 | async-start | bytes 3649536 | tf_op jit(solution)/shard_map/all_gather | solution.py:53
  7.9 122.0 %all-gather.8.cloned.1.call-start = ((), (), s32[]{:S(2)}) async-start(), calls=%async_computation.9 | async-start | bytes 1216512 | tf_op jit(solution)/shard_map/all_gather | solution.py:54
  8.7 325.0 %all-gather.10.cloned.1.call-start = ((), (), s32[]{:S(2)}) async-start(), calls=%async_computation.10 | async-start | bytes 11796480 | tf_op jit(solution)/shard_map/all_gather | solution.py:58
  9.4 357.2 %all-gather.12.cloned.1.call-start = ((), (), s32[]{:S(2)}) async-start(), calls=%async_computation.11 | async-start | bytes 11796480 | tf_op jit(solution)/shard_map/all_gather | solution.py:59
  11.0 14.1 %copy-start.43 = (f32[1,2,2,128]{3,1,2,0:T(2,128)}, f32[1,2,2,128]{3,1,2,0:T(2,128)S(1)}, u32[]{:S(2)}) copy-start(f32[1,2,2,128]{3,1,2,0:T(2,128)S(1)} %copy.176) | copy-start | bytes 6148
  11.0 21.5 %copy-start.41 = (f32[512]{0:T(512)}, f32[512]{0:T(512)S(1)}, u32[]{:S(2)}) copy-start(f32[512]{0:T(512)S(1)} %rsqrt.22) | copy-start | bytes 6148
  12.2 12.8 %copy-start.30 = (s32[256,256]{0,1:T(8,128)}, s32[256,256]{0,1:T(8,128)S(1)}, u32[]{:S(2)}) copy-start(s32[256,256]{0,1:T(8,128)S(1)} %copy.125) | copy-start | bytes 786436
  102.5 27.4 %copy-start.16 = (bf16[2,256,768]{2,1,0:T(8,128)(2,1)S(1)}, bf16[2,256,768]{2,1,0:T(8,128)(2,1)}, u32[]{:S(2)}) copy-start(bf16[2,256,768]{2,1,0:T(8,128)(2,1)} %param.13) | copy-start | bytes 2359300
  103.3 30.0 %copy-start.37 = (f32[768]{0:T(1024)S(1)}, f32[768]{0:T(1024)}, u32[]{:S(2)}) copy-start(f32[768]{0:T(1024)} %param.18) | copy-start | bytes 9220
  103.5 29.2 %copy-start.26 = (bf16[96,8,2,256]{3,1,2,0:T(8,128)(2,1)}, bf16[96,8,2,256]{3,1,2,0:T(8,128)(2,1)S(1)}, u32[]{:S(2)}) copy-start(bf16[96,8,2,256]{3,1,2,0:T(8,128)(2,1)S(1)} %copy.177) | copy-start | bytes 2359300
  141.3 116.4 %copy-start.28 = (bf16[2,256,768]{2,1,0:T(8,128)(2,1)S(1)}, bf16[2,256,768]{2,1,0:T(8,128)(2,1)}, u32[]{:S(2)}) copy-start(bf16[2,256,768]{2,1,0:T(8,128)(2,1)} %param.25) | copy-start | bytes 2359300
  141.3 133.7 %all-to-all-start = ((bf16[2,16,48,768]{3,2,0,1:T(8,128)(2,1)}), bf16[2,16,48,768]{3,2,0,1:T(8,128)(2,1)}, u32[]{:S(2)}, u32[]{:S(2)}) async-start(bf16[2,16,48,768]{3,2,0,1:T(8,128)(2,1)} %copy.134), calls=%async_computation | async-start | bytes 4718592 | tf_op jit(solution)/shard_map/all_to_all | solution.py:119
  275.0 55.4 %all-to-all-start.2 = ((bf16[2,16,48,768]{3,2,0,1:T(8,128)(2,1)}), bf16[2,16,48,768]{3,2,0,1:T(8,128)(2,1)}, u32[]{:S(2)}, u32[]{:S(2)}) async-start(bf16[2,16,48,768]{3,2,0,1:T(8,128)(2,1)} %copy.140), calls=%async_computation.2 | async-start | bytes 4718592 | tf_op jit(solution)/shard_map/all_to_all | solution.py:154
  279.4 387.1 %reduce-scatter.12.cloned.1.call-start = ((), (), s32[]{:S(2)}) async-start(), calls=%async_computation.15 | async-start | bytes 11796480 | tf_op jit(solution)/shard_map/reduce_scatter | solution.py:174
  333.7 15.6 %copy-start.33 = (bf16[2,8,2,48,768]{4,3,1,0,2:T(8,128)(2,1)S(1)}, bf16[2,8,2,48,768]{4,3,1,0,2:T(8,128)(2,1)}, u32[]{:S(2)}) copy-start(bf16[2,8,2,48,768]{4,3,1,0,2:T(8,128)(2,1)} %copy.141) | copy-start | bytes 7077892
  366.2 304.6 %reduce-scatter.10.cloned.1.call-start = ((), (), s32[]{:S(2)}) async-start(), calls=%async_computation.14 | async-start | bytes 11796480 | tf_op jit(solution)/shard_map/reduce_scatter | solution.py:171
  366.6 24.2 %copy-start.32 = (bf16[2,8,2,48,768]{4,3,1,0,2:T(8,128)(2,1)S(1)}, bf16[2,8,2,48,768]{4,3,1,0,2:T(8,128)(2,1)}, u32[]{:S(2)}) copy-start(bf16[2,8,2,48,768]{4,3,1,0,2:T(8,128)(2,1)} %copy.135) | copy-start | bytes 7077892
  423.7 58.1 %all-to-all-start.1 = ((bf16[2,2,384,768]{3,0,1,2:T(2,128)(2,1)}), bf16[2,2,384,768]{3,0,1,2:T(2,128)(2,1)}, u32[]{:S(2)}, u32[]{:S(2)}) async-start(bf16[2,2,384,768]{3,0,1,2:T(2,128)(2,1)} %copy.136), calls=%async_computation.1 | async-start | bytes 4718592 | tf_op jit(solution)/shard_map/all_to_all | solution.py:125
  481.8 57.8 %all-to-all-start.3 = ((bf16[2,2,384,768]{3,0,1,2:T(2,128)(2,1)}), bf16[2,2,384,768]{3,0,1,2:T(2,128)(2,1)}, u32[]{:S(2)}, u32[]{:S(2)}) async-start(bf16[2,2,384,768]{3,0,1,2:T(2,128)(2,1)} %copy.142), calls=%async_computation.3 | async-start | bytes 4718592 | tf_op jit(solution)/shard_map/all_to_all | solution.py:162
  486.2 193.0 %reduce-scatter.8.cloned.1.call-start = ((), (), s32[]{:S(2)}) async-start(), calls=%async_computation.13 | async-start | bytes 2433024 | tf_op jit(solution)/shard_map/reduce_scatter | solution.py:230
  497.8 43.9 %copy-start.6 = (bf16[2,512,16,48]{1,3,2,0:T(8,128)(2,1)S(1)}, bf16[2,512,16,48]{1,3,2,0:T(8,128)(2,1)}, u32[]{:S(2)}) copy-start(bf16[2,512,16,48]{1,3,2,0:T(8,128)(2,1)} %multiply_convert_fusion.2) | copy-start | bytes 4718596
  556.5 16.4 %copy-start.29 = (bf16[2,256,768]{2,1,0:T(8,128)(2,1)S(1)}, bf16[2,256,768]{2,1,0:T(8,128)(2,1)}, u32[]{:S(2)}) copy-start(bf16[2,256,768]{2,1,0:T(8,128)(2,1)} %param.25) | copy-start | bytes 2359300
  580.9 223.5 %reduce-scatter.6.cloned.1.call-start = ((), (), s32[]{:S(2)}) async-start(), calls=%async_computation.12 | async-start | bytes 7299072 | tf_op jit(solution)/shard_map/reduce_scatter | solution.py:229
  585.8 7.9 slice-start
  610.7 7.6 copy-start.42
  610.7 7.6 copy-start.46
  610.7 7.6 copy-start.17
  618.4 45.3 %copy-start.44 = (f32[1,2,2,128]{3,1,2,0:T(2,128)S(1)}, f32[1,2,2,128]{3,1,2,0:T(2,128)}, u32[]{:S(2)}) copy-start(f32[1,2,2,128]{3,1,2,0:T(2,128)} %copy-done.43) | copy-start | bytes 6148
  618.4 45.3 %copy-start.10 = (f32[512,768]{1,0:T(8,128)S(1)}, f32[512,768]{1,0:T(8,128)}, u32[]{:S(2)}) copy-start(f32[512,768]{1,0:T(8,128)} %copy-done.9) | copy-start | bytes 4718596
  618.4 45.3 %copy-start.18 = (bf16[2,256,768]{2,1,0:T(8,128)(2,1)S(1)}, bf16[2,256,768]{2,1,0:T(8,128)(2,1)}, u32[]{:S(2)}) copy-start(bf16[2,256,768]{2,1,0:T(8,128)(2,1)} %param.13) | copy-start | bytes 2359300
  666.5 137.9 %copy-start.1 = (f32[32,12]{0,1:T(8,128)S(1)}, f32[32,12]{0,1:T(8,128)}, u32[]{:S(2)}) copy-start(f32[32,12]{0,1:T(8,128)} %param.17) | copy-start | bytes 4612
  (35 other events, 107.0 us)
Sparse Core Ops, SparseCore 0:
  11.0 62.8 all-gather.5
  76.9 52.9 all-gather.7
  131.5 63.2 all-gather.9
  196.2 64.7 all-gather.11
  366.3 76.2 reduce-scatter.11
  445.0 78.3 reduce-scatter.9
  581.0 98.1 reduce-scatter.7
  686.4 117.9 reduce-scatter.5
where the time goes:
time: 816 us; the launch traced here: 811 us
  waiting for transfers between devices  322 us (39%)
  matrix products  161 us (20%)
  blocking collectives  151 us (19%)
  local copies, waits for them, and re-layouts  94.6 us (12%)
  other arithmetic  48.7 us (6%)
  starting transfers between devices  18.6 us (2%)
  between operations  15.4 us (2%)
    reduce_scatter x1, waiting for transfers between devices, on_device(): lax.psum_scatter(qkv_part, ('dp', 'expert'), scatter_dimension=0, tiled=T...  125 us
    all_gather x1, blocking collectives, on_device(): lax.all_gather(router_weight, ('dp', 'expert'), axis=0, tiled=True)  112 us
    all_to_all x1, waiting for transfers between devices, on_device(): lax.all_to_all(grad_send, 'expert', split_axis=1, concat_axis=2, tiled=True)  47.7 us
    all_to_all x1, waiting for transfers between devices, on_device(): lax.all_to_all(grad_in_rows, 'expert', split_axis=2, concat_axis=1, tiled...  41.8 us
    psum x1, blocking collectives, on_device(): lax.psum((gain_attn_part, table_part, gain_ffn_part), ('dp', 'expert'))  39.1 us
    all_gather x1, waiting for transfers between devices, on_device(): lax.all_gather(qkv_weight, ('dp', 'expert'), axis=0, tiled=True)  37.4 us
    all_to_all x1, waiting for transfers between devices, on_device(): lax.all_to_all(produced, 'expert', split_axis=2, concat_axis=1, tiled=True)  36.9 us
    all_gather x1, waiting for transfers between devices, on_device(): lax.all_gather(out_weight, ('dp', 'expert'), axis=0, tiled=True)  26.4 us
  transfers between devices with their start and end apart: 12, of which 7 were waited for; matrix products, arithmetic and copies ran while one was open for 37% of the time, Pallas kernels for 0%

commit v1 on v0

v1 whole, which is shorter than its diff:
```python
import functools

import jax
import jax.numpy as jnp
from jax import lax
from jax.sharding import PartitionSpec as P

EPSILON = 1e-06
HIGHEST = lax.Precision.HIGHEST


def rms_norm(values, gain_vec):
    return (
        values * lax.rsqrt(jnp.mean(values * values, axis=-1, keepdims=True) + EPSILON) * gain_vec
    )


def gelu_tanh(values):
    return jax.nn.gelu(values, approximate=True)


def attention_scores(queries, key_rows, bias_full, allowed, score_scale):
    scores = (
        jnp.einsum("mqhd,mkhd->mhqk", queries, key_rows, preferred_element_type=jnp.float32)
        * score_scale
        + bias_full[None]
    )
    return jnp.where(allowed[:, None], scores, -1e30)


def flip_pairs(size, bit):
    return [(i, i ^ bit) for i in range(size)]


def bits_of(size):
    return [1 << i for i in range(size.bit_length() - 1)]


def gather_relative(block, size):
    blocks = [block]
    for bit in reversed(bits_of(size)):
        blocks = blocks + [lax.ppermute(b, "dp", flip_pairs(size, bit)) for b in blocks]
    return blocks


def scatter_relative(parts, size):
    for bit in bits_of(size):
        half = len(parts) // 2
        arrived = [
            lax.ppermute(p.astype(jnp.bfloat16), "dp", flip_pairs(size, bit)) for p in parts[half:]
        ]
        parts = [p.astype(jnp.float32) + q.astype(jnp.float32) for p, q in zip(parts[:half], arrived)]
    return parts[0]


def halving_scatter(matrix, sizes, order):
    axis_bits = [("dp", b) for b in reversed(bits_of(sizes["dp"]))]
    axis_bits += [("expert", b) for b in reversed(bits_of(sizes["expert"]))]
    blocks = sizes["dp"] * sizes["expert"]
    rows, columns = matrix.shape
    held = matrix.reshape((2,) * len(axis_bits) + (rows // blocks, columns))
    left = list(axis_bits)
    for axis, bit in order:
        place = left.index((axis, bit))
        left.pop(place)
        mine = (lax.axis_index(axis) // bit) % 2
        keep = lax.dynamic_index_in_dim(held, mine, place, keepdims=False)
        send = lax.dynamic_index_in_dim(held, 1 - mine, place, keepdims=False)
        arrived = lax.ppermute(send.astype(jnp.bfloat16), axis, flip_pairs(sizes[axis], bit))
        held = keep.astype(jnp.float32) + arrived.astype(jnp.float32)
    return held


def butterfly_sum(values, sizes):
    for axis in ("dp", "expert"):
        for bit in bits_of(sizes[axis]):
            values = values + lax.ppermute(values, axis, flip_pairs(sizes[axis], bit))
    return values


def gelu_slope(values, upstream):
    return jax.vjp(gelu_tanh, values)[1](upstream)[0]


def dot_nn(a, b):
    return lax.dot_general(a, b, (((1,), (0,)), ((), ())), preferred_element_type=jnp.float32)


def dot_nt(a, b):
    return lax.dot_general(a, b, (((1,), (1,)), ((), ())), preferred_element_type=jnp.float32)


def dot_tn(a, b):
    return lax.dot_general(a, b, (((0,), (0,)), ((), ())), preferred_element_type=jnp.float32)


def on_device(
    sizes,
    tokens,
    gain_attn,
    qkv_weight,
    out_weight,
    bias_table,
    gain_ffn,
    router_weight,
    expert_in,
    expert_out,
    lengths,
    buckets,
    routes,
    cotangent,
):
    micro, tok_mb, model_width = tokens.shape
    experts = router_weight.shape[1]
    capacity = 3 * tok_mb // experts
    bucket_count, head_count = bias_table.shape
    head_size = model_width // head_count
    score_scale = head_size ** (-0.5)
    row_count = micro * tok_mb
    local_experts = experts // sizes["expert"]
    orders = (
        [("dp", 1), ("expert", 1)]
        + [("dp", b) for b in reversed(bits_of(sizes["dp"])) if b > 1]
        + [("expert", b) for b in reversed(bits_of(sizes["expert"])) if b > 1],
        [("dp", 1)]
        + [("dp", b) for b in reversed(bits_of(sizes["dp"])) if b > 1]
        + [("expert", 1)]
        + [("expert", b) for b in reversed(bits_of(sizes["expert"])) if b > 1],
    )
    packed = jnp.concatenate(
        [qkv_weight, out_weight, jnp.pad(router_weight, ((0, 0), (0, -experts % 128)))], axis=1
    )
    packed_full = lax.all_gather(packed, ("dp", "expert"), axis=0, tiled=True)
    qkv_full = packed_full[:, : 3 * model_width]
    out_full = packed_full[:, 3 * model_width : 4 * model_width]
    router_full = packed_full[:, 4 * model_width : 4 * model_width + experts]
    in_blocks = gather_relative(expert_in, sizes["dp"])
    back_blocks = gather_relative(expert_out, sizes["dp"])
    flat_x = tokens.astype(jnp.float32).reshape(row_count, model_width)
    normed_low = rms_norm(flat_x, gain_attn).astype(jnp.bfloat16)
    qkv_act = jnp.dot(normed_low, qkv_full, preferred_element_type=jnp.float32).astype(jnp.bfloat16)
    queries = qkv_act[:, :model_width].reshape(micro, tok_mb, head_count, head_size)
    key_rows = qkv_act[:, model_width : 2 * model_width].reshape(
        micro, tok_mb, head_count, head_size
    )
    value_rows = qkv_act[:, 2 * model_width :].reshape(micro, tok_mb, head_count, head_size)
    positions = jnp.arange(tok_mb, dtype=jnp.int32)
    seq_ends = jnp.cumsum(lengths[:, 0, :], axis=1)
    segment = jnp.sum((positions[None, :, None] >= seq_ends[:, None, :]).astype(jnp.int32), axis=2)
    allowed = (positions[:, None] >= positions[None, :])[None] & (
        segment[:, :, None] == segment[:, None, :]
    )
    distance = jnp.maximum(positions[:, None] - positions[None, :], 0)
    bucket_ids = jnp.arange(bucket_count, dtype=jnp.int32)
    thresholds = jnp.sum((buckets[None, :] < bucket_ids[:, None]).astype(jnp.int32), axis=1)
    distance_bucket = jnp.sum(
        (distance[:, :, None] >= thresholds[1:][None, None, :]).astype(jnp.int32), axis=2
    )
    bucket_hot = (distance_bucket[:, :, None] == bucket_ids).astype(jnp.float32)
    bias_full = jnp.einsum("qkb,bh->hqk", bucket_hot, bias_table, precision=HIGHEST)
    scores = attention_scores(queries, key_rows, bias_full, allowed, score_scale)
    row_max = jnp.max(scores, axis=-1, keepdims=True)
    row_sum = jnp.sum(jnp.exp(scores - row_max), axis=-1, keepdims=True)
    log_total = row_max + jnp.log(row_sum)
    probability = jnp.exp(scores - log_total)
    context = jnp.einsum(
        "mhqk,mkhd->mqhd",
        probability.astype(jnp.bfloat16),
        value_rows,
        preferred_element_type=jnp.float32,
    )
    context = context.reshape(row_count, model_width).astype(jnp.bfloat16)
    middle = flat_x + jnp.dot(context, out_full, preferred_element_type=jnp.float32)
    ffn_low = rms_norm(middle, gain_ffn).astype(jnp.bfloat16)
    logits = jnp.dot(ffn_low, router_full, preferred_element_type=jnp.float32)
    grad_out = cotangent.astype(jnp.float32).reshape(row_count, model_width)
    expert_ids = jnp.arange(experts, dtype=jnp.int32)
    flat_routes = routes.reshape(row_count, 2)
    route_hot = (flat_routes[:, :, None] == expert_ids).astype(jnp.float32)
    token_hits = jnp.sum(route_hot, axis=1)
    chosen = jnp.sum(route_hot * logits[:, None, :], axis=2)
    gate_weights = jax.nn.softmax(chosen, axis=-1)
    rows_at = jnp.arange(row_count, dtype=jnp.int32)
    micro_at = rows_at // tok_mb
    before = (
        (rows_at[None, :] < rows_at[:, None]) & (micro_at[None, :] == micro_at[:, None])
    ).astype(jnp.bfloat16)
    earlier = jnp.dot(before, token_hits.astype(jnp.bfloat16), preferred_element_type=jnp.float32)
    rank = jnp.sum(route_hot * earlier[:, None, :], axis=2).astype(jnp.int32)
    group_rows = micro * capacity
    slot_rows = sizes["expert"] * group_rows
    column = (
        (flat_routes % local_experts) * slot_rows
        + (flat_routes // local_experts) * group_rows
        + micro_at[:, None] * capacity
        + rank
    )
    columns_at = jnp.arange(local_experts * slot_rows, dtype=jnp.int32)
    first_hot = column[:, 0:1] == columns_at[None, :]
    second_hot = column[:, 1:2] == columns_at[None, :]
    slot_hot = (first_hot | second_hot).astype(jnp.bfloat16)
    gated_hot = jnp.where(
        first_hot, gate_weights[:, 0:1], jnp.where(second_hot, gate_weights[:, 1:2], 0.0)
    ).astype(jnp.bfloat16)
    cotangent_rows = cotangent.reshape(row_count, model_width)

    def exchange(values):
        sent = values.reshape((sizes["expert"], group_rows) + values.shape[1:])
        got = lax.all_to_all(sent, "expert", split_axis=0, concat_axis=0, tiled=True)
        return got.reshape(values.shape)

    spans = [slice(e * slot_rows, (e + 1) * slot_rows) for e in range(local_experts)]
    received, grad_recv = [], []
    for span in spans:
        received.append(exchange(dot_tn(slot_hot[:, span], ffn_low).astype(jnp.bfloat16)))
        grad_recv.append(
            exchange(dot_tn(gated_hot[:, span], cotangent_rows).astype(jnp.bfloat16))
        )
    produced, grad_back, gate_terms, in_grads, out_grads = [], [], [], [], []
    for e in range(local_experts):
        in_full = jnp.concatenate([b[e] for b in in_blocks], axis=1)
        back_full = jnp.concatenate([b[e] for b in back_blocks], axis=0)
        block_width = expert_in.shape[2]
        pre_act = dot_nn(received[e], in_full)
        hidden = gelu_tanh(pre_act).astype(jnp.bfloat16)
        made = dot_nn(hidden, back_full).astype(jnp.bfloat16)
        gate_terms.append(
            jnp.sum(grad_recv[e].astype(jnp.float32) * made.astype(jnp.float32), axis=1)
        )
        grad_pre = gelu_slope(pre_act, dot_nt(grad_recv[e], back_full)).astype(jnp.bfloat16)
        grad_rows = dot_nt(grad_pre, in_full).astype(jnp.bfloat16)
        grad_back.append(exchange(grad_rows))
        produced.append(made)
        cuts = [slice(r * block_width, (r + 1) * block_width) for r in range(sizes["dp"])]
        out_grads.append(
            scatter_relative([dot_tn(hidden[:, c], grad_recv[e]) for c in cuts], sizes["dp"])
        )
        in_grads.append(
            scatter_relative([dot_tn(received[e], grad_pre[:, c]) for c in cuts], sizes["dp"])
        )
    expert_in_grad = jnp.stack(in_grads)
    expert_out_grad = jnp.stack(out_grads)
    terms = jnp.stack([t.reshape(sizes["expert"], group_rows) for t in gate_terms], axis=1)
    terms = lax.all_to_all(terms, "expert", split_axis=0, concat_axis=0, tiled=True)
    terms = jnp.transpose(terms, (1, 0, 2)).reshape(1, local_experts * slot_rows)
    returned = [exchange(made) for made in produced]
    mixture = sum(dot_nn(gated_hot[:, s], r) for s, r in zip(spans, returned))
    block_out = (middle + mixture).astype(jnp.bfloat16).reshape(tokens.shape)
    grad_ffn = sum(dot_nn(slot_hot[:, s], r) for s, r in zip(spans, grad_back))
    first_term = jnp.sum(jnp.where(first_hot, terms, 0.0), axis=1, keepdims=True)
    second_term = jnp.sum(jnp.where(second_hot, terms, 0.0), axis=1, keepdims=True)
    lean = gate_weights[:, 1:2] * first_term - gate_weights[:, 0:1] * second_term
    grad_logits = (lean * (route_hot[:, 0] - route_hot[:, 1])).astype(jnp.bfloat16)
    router_part = dot_tn(ffn_low, grad_logits)
    grad_ffn = grad_ffn + dot_nt(grad_logits, router_full)
    grad_mid_part, gain_ffn_part = jax.vjp(rms_norm, middle, gain_ffn)[1](grad_ffn)
    grad_middle = grad_out + grad_mid_part
    grad_attn = grad_middle.astype(jnp.bfloat16)
    out_part = jnp.einsum("nc,nd->cd", context, grad_attn, preferred_element_type=jnp.float32)
    grad_context = jnp.einsum(
        "nd,cd->nc", grad_attn, out_full, preferred_element_type=jnp.float32
    ).astype(jnp.bfloat16)
    grad_context = grad_context.reshape(micro, tok_mb, head_count, head_size)
    scores_again = attention_scores(queries, key_rows, bias_full, allowed, score_scale)
    prob_again = jnp.exp(scores_again - log_total)
    grad_prob = jnp.einsum(
        "mqhd,mkhd->mhqk", grad_context, value_rows, preferred_element_type=jnp.float32
    )
    row_delta = jnp.sum(prob_again * grad_prob, axis=-1, keepdims=True)
    grad_scores = (prob_again * (grad_prob - row_delta)).astype(jnp.bfloat16)
    score_total = jnp.sum(grad_scores.astype(jnp.float32), axis=0)
    table_part = jnp.einsum("hqk,qkb->bh", score_total, bucket_hot, precision=HIGHEST)
    grad_queries = (
        jnp.einsum("mhqk,mkhd->mqhd", grad_scores, key_rows, preferred_element_type=jnp.float32)
        * score_scale
    )
    grad_keys = (
        jnp.einsum("mhqk,mqhd->mkhd", grad_scores, queries, preferred_element_type=jnp.float32)
        * score_scale
    )
    grad_values = jnp.einsum(
        "mhqk,mqhd->mkhd",
        prob_again.astype(jnp.bfloat16),
        grad_context,
        preferred_element_type=jnp.float32,
    )
    grad_qkv = jnp.concatenate(
        [
            grad_queries.reshape(row_count, model_width),
            grad_keys.reshape(row_count, model_width),
            grad_values.reshape(row_count, model_width),
        ],
        axis=1,
    ).astype(jnp.bfloat16)
    qkv_part = jnp.einsum("nc,nd->cd", normed_low, grad_qkv, preferred_element_type=jnp.float32)
    grad_normed = jnp.einsum("nd,cd->nc", grad_qkv, qkv_full, preferred_element_type=jnp.float32)
    grad_x_part, gain_attn_part = jax.vjp(rms_norm, flat_x, gain_attn)[1](grad_normed)
    tokens_grad = (grad_middle + grad_x_part).astype(jnp.bfloat16).reshape(tokens.shape)
    split = 3 * model_width // 2
    early = halving_scatter(jnp.concatenate([out_part, router_part], axis=1), sizes, orders[0])
    out_grad, router_grad = early[:, :model_width], early[:, model_width:]
    qkv_grad = jnp.concatenate(
        [
            halving_scatter(qkv_part[:, :split], sizes, orders[0]),
            halving_scatter(qkv_part[:, split:], sizes, orders[1]),
        ],
        axis=1,
    )
    small = butterfly_sum(
        jnp.concatenate([gain_attn_part, gain_ffn_part, table_part.reshape(-1)]), sizes
    )
    gain_attn_grad = small[:model_width]
    gain_ffn_grad = small[model_width : 2 * model_width]
    table_grad = small[2 * model_width :].reshape(bias_table.shape)
    return (
        block_out,
        tokens_grad,
        gain_attn_grad,
        qkv_grad,
        out_grad,
        table_grad,
        gain_ffn_grad,
        router_grad,
        expert_in_grad,
        expert_out_grad,
    )


def solution(mesh):
    sizes = {"dp": mesh.shape["dp"], "expert": mesh.shape["expert"]}
    return jax.shard_map(
        functools.partial(on_device, sizes),
        mesh=mesh,
        in_specs=(
            P(None, ("dp", "expert"), None),
            P(),
            P(("dp", "expert"), None),
            P(("dp", "expert"), None),
            P(),
            P(),
            P(("dp", "expert"), None),
            P("expert", None, "dp"),
            P("expert", "dp", None),
            P(None, ("dp", "expert"), None),
            P(),
            P(None, ("dp", "expert"), None),
            P(None, ("dp", "expert"), None),
        ),
        out_specs=(
            P(None, ("dp", "expert"), None),
            P(None, ("dp", "expert"), None),
            P(),
            P(("dp", "expert"), None),
            P(("dp", "expert"), None),
            P(),
            P(),
            P(("dp", "expert"), None),
            P("expert", None, "dp"),
            P("expert", "dp", None),
        ),
        check_vma=False,
    )
```

time: 816 us -> 656 us (0.80)
  blocking collectives: 151 us -> 0 us
  waiting for transfers between devices: 322 us -> 214 us
  starting transfers between devices: 18.6 us -> 75.3 us
  matrix products: 161 us -> 201 us
    ppermute x0 -> x38, waiting for transfers between devices: none -> 144 us  [the longest x6 81.2 us: gather_relative(): lax.ppermute(b, 'dp', flip_pairs(size, bit))]
    reduce_scatter x4 -> x0, waiting for transfers between devices: 129 us -> none  [the longest x1 125 us: on_device(): lax.psum_scatter(qkv_part, ('dp', 'expert'), scatter_dimension=0, tiled=T...]
    all_gather x1 -> x0, blocking collectives: 112 us -> none  [on_device(): lax.all_gather(router_weight, ('dp', 'expert'), axis=0, tiled=True)]
    all_gather x4 -> x1, waiting for transfers between devices: 63.8 us -> 0.01 us  [on_device(): packed_full = lax.all_gather(packed, ('dp', 'expert'), axis=0, tiled=True)]
    all_to_all x4 -> x9, waiting for transfers between devices: 126 us -> 70 us  [the longest x8 67.9 us: exchange(): lax.all_to_all(sent, 'expert', split_axis=0, concat_axis=0, tiled=True)]
    dot_general x15 -> x37, matrix products: 120 us -> 164 us  [the longest x21 67.1 us: dot_tn(): lax.dot_general(a, b, (((0,), (0,)), ((), ())), preferred_element_type=jn...]
    psum x1 -> x0, blocking collectives: 39.1 us -> none  [on_device(): lax.psum((gain_attn_part, table_part, gain_ffn_part), ('dp', 'expert'))]
    ppermute x0 -> x38, starting transfers between devices: none -> 32.6 us  [the longest x15 21.1 us: halving_scatter(): lax.ppermute(send.astype(jnp.bfloat16), axis, flip_pairs(sizes[axis], bit))]
  transfers between devices with their start and end apart: 12 -> 48, of which waited for: 7 -> 24; matrix products, arithmetic and copies ran while one was open for 37% -> 45% of each run, Pallas kernels for 0% -> 0%
where the time goes in v1:
time: 656 us; the launch traced here: 645 us
  waiting for transfers between devices  214 us (33%)
  matrix products  201 us (31%)
  local copies, waits for them, and re-layouts  95.1 us (14%)
  starting transfers between devices  75.3 us (11%)
  other arithmetic  43.9 us (7%)
  between operations  15.8 us (2%)
    ppermute x6, waiting for transfers between devices, gather_relative(): lax.ppermute(b, 'dp', flip_pairs(size, bit))  81.2 us
    all_to_all x8, waiting for transfers between devices, exchange(): lax.all_to_all(sent, 'expert', split_axis=0, concat_axis=0, tiled=True)  67.9 us
    dot_general x21, matrix products, dot_tn(): lax.dot_general(a, b, (((0,), (0,)), ((), ())), preferred_element_type=jn...  67.1 us
    dot_general x8, matrix products, dot_nn(): lax.dot_general(a, b, (((1,), (0,)), ((), ())), preferred_element_type=jn...  45.7 us
    dot_general x5, matrix products, dot_nt(): lax.dot_general(a, b, (((1,), (1,)), ((), ())), preferred_element_type=jn...  42.8 us
    all_to_all x8, starting transfers between devices, exchange(): lax.all_to_all(sent, 'expert', split_axis=0, concat_axis=0, tiled=True)  39.2 us
    ppermute x12, waiting for transfers between devices, scatter_relative(): lax.ppermute(p.astype(jnp.bfloat16), 'dp', flip_pairs(size, bit))  31 us
    ppermute x15, waiting for transfers between devices, halving_scatter(): lax.ppermute(send.astype(jnp.bfloat16), axis, flip_pairs(sizes[axis], bit))  24.9 us
  transfers between devices with their start and end apart: 48, of which 24 were waited for; matrix products, arithmetic and copies ran while one was open for 45% of the time, Pallas kernels for 0%

profile of v1, /device:TPU:0, one launch (start us, length us, event | category | flops | bytes accessed | tf_op | source)
XLA Modules:
  0.0 645.1 jit_solution(5448946916791296132)
XLA Ops:
  19.1 11.6 %copy.124 = pred[256,256,32]{1,2,0:T(32,128)(4,1)S(1)} copy(pred[256,256,32]{0,2,1:T(32,128)(4,1)S(1)} %iota_compare_fusion) | data formatting | bytes 4194304 | tf_op jit(solution)/shard_map/eq | solution.py:159
  45.6 30.9 %collective-permute-done = bf16[2,768,768]{2,1,0:T(8,128)(2,1)} collective-permute-done((bf16[2,768,768]{2,1,0:T(8,128)(2,1)}, bf16[2,768,768]{2,1,0:T(8,128)(2,1)}, u32[]{:S(2)}, u32[]{:S(2)}) %collective-permute-start) | collective-permute-done | bytes 2359328 | tf_op jit(solution)/shard_map/ppermute | solution.py:42
  76.6 50.3 %collective-permute-done.3 = bf16[2,768,768]{2,1,0:T(8,128)(2,1)} collective-permute-done((bf16[2,768,768]{2,1,0:T(8,128)(2,1)}, bf16[2,768,768]{2,1,0:T(8,128)(2,1)}, u32[]{:S(2)}, u32[]{:S(2)}) %collective-permute-start.3) | collective-permute-done | bytes 2359328 | tf_op jit(solution)/shard_map/ppermute | solution.py:42
  169.9 6.0 all-to-all-start
  190.1 15.2 %all-to-all-done = bf16[8,96,768]{2,1,0:T(8,128)(2,1)} async-done(((bf16[8,96,768]{2,1,0:T(8,128)(2,1)}), bf16[8,96,768]{2,1,0:T(8,128)(2,1)}, u32[]{:S(2)}, u32[]{:S(2)}) %all-to-all-start) | async-done | bytes 1179680 | tf_op jit(solution)/shard_map/all_to_all | solution.py:209
  205.3 4.2 all-to-all-start.4
  217.1 10.5 %multiply_convert_fusion.1 = (bf16[768,3072]{1,0:T(8,128)(2,1)}, f32[768,3072]{1,0:T(8,128)}) fusion(bf16[768,768]{1,0:T(8,128)(2,1)} %bitcast.11, bf16[768,768]{1,0:T(8,128)(2,1)S(1)} %copy-done.66, bf16[768,768]{1,0:T(8,128)(2,1)S(1)} %copy-done.63, bf16[768,768]{1,0:T(8,128)(2,1)S(1)} %copy-done.58, bf16[768,768]{1,0:T(8,128)(2,1)S(1)} %copy-done.54), kind=kOutput, calls=%fused_computation.19 | convolution fusion | flops 3663986688 | bytes 20054016 | tf_op jit(solution)/shard_map/dot_general | solution.py:86
  227.6 10.4 %all-to-all-done.4 = bf16[8,96,768]{2,1,0:T(8,128)(2,1)} async-done(((bf16[8,96,768]{2,1,0:T(8,128)(2,1)}), bf16[8,96,768]{2,1,0:T(8,128)(2,1)}, u32[]{:S(2)}, u32[]{:S(2)}) %all-to-all-start.4) | async-done | bytes 1179680 | tf_op jit(solution)/shard_map/all_to_all | solution.py:209
  241.8 14.1 %fusion.6 = bf16[768,3072]{1,0:T(8,128)(2,1)S(1)} fusion(f32[768,3072]{1,0:T(8,128)} %get-tuple-element.92, bf16[768,768]{1,0:T(8,128)(2,1)} %bitcast.37, bf16[768,768]{1,0:T(8,128)(2,1)} %get-tuple-element.69, bf16[768,768]{1,0:T(8,128)(2,1)} %get-tuple-element.67, bf16[768,768]{1,0:T(8,128)(2,1)} %get-tuple-element.65, bf16[768,768]{1,0:T(8,128)(2,1)S(1)} %copy-done.48), kind=kOutput, calls=%fused_computation.10 | convolution fusion | flops 3689938944 | bytes 20054016 | tf_op jit(solution)/shard_map/dot_general | solution.py:90
  255.9 4.5 convolution_convert_fusion.7
  270.9 5.1 convolution_convert_fusion.11
  276.0 6.2 all-to-all-start.6
  286.5 4.3 fusion.69
  290.8 9.4 %multiply_convert_fusion = (bf16[768,3072]{1,0:T(8,128)(2,1)}, f32[768,3072]{1,0:T(8,128)}) fusion(bf16[768,768]{1,0:T(8,128)(2,1)S(1)} %bitcast.269, bf16[768,768]{1,0:T(8,128)(2,1)S(1)} %copy-done.56, bf16[768,768]{1,0:T(8,128)(2,1)S(1)} %copy-done.52, bf16[768,768]{1,0:T(8,128)(2,1)S(1)} %copy-done.45, bf16[768,768]{1,0:T(8,128)(2,1)S(1)} %copy-done.43), kind=kOutput, calls=%fused_computation.18 | convolution fusion | flops 3663986688 | bytes 20054016 | tf_op jit(solution)/shard_map/dot_general | solution.py:86
  300.2 10.4 %all-to-all-done.6 = bf16[8,96,768]{2,1,0:T(8,128)(2,1)S(1)} async-done(((bf16[8,96,768]{2,1,0:T(8,128)(2,1)}), bf16[8,96,768]{2,1,0:T(8,128)(2,1)S(1)}, u32[]{:S(2)}, u32[]{:S(2)}) %all-to-all-start.6) | async-done | bytes 1179680 | tf_op jit(solution)/shard_map/all_to_all | solution.py:209
  310.6 14.8 %fusion.13 = bf16[768,3072]{1,0:T(8,128)(2,1)S(1)} fusion(f32[768,3072]{1,0:T(8,128)} %get-tuple-element.94, bf16[768,768]{1,0:T(8,128)(2,1)S(1)} %bitcast.274, bf16[768,768]{1,0:T(8,128)(2,1)} %get-tuple-element.68, bf16[768,768]{1,0:T(8,128)(2,1)} %get-tuple-element.66, bf16[768,768]{1,0:T(8,128)(2,1)} %get-tuple-element.64, ...), kind=kOutput, calls=%fused_computation.17 | convolution fusion | flops 3689938944 | bytes 20054016 | tf_op jit(solution)/shard_map/dot_general | solution.py:90
  332.4 6.1 multiply_reduce_fusion.2
  342.6 7.6 %multiply_reduce_fusion.1 = (f32[768]{0:T(1024)S(1)}, bf16[768,768]{1,0:T(8,128)(2,1)}) fusion(bf16[8,96,768]{2,1,0:T(8,128)(2,1)S(1)} %all-to-all-done.6, bf16[768,3072]{1,0:T(8,128)(2,1)} %get-tuple-element.93, bf16[768,768]{1,0:T(8,128)(2,1)S(1)} %copy-done.62, bf16[768,768]{1,0:T(8,128)(2,1)S(1)} %copy-done.60, bf16[768,768]{1,0:T(8,128)(2,1)S(1)} %copy-done.50, ...), kind=kOutput, calls=%fused_computation.58 | convolution fusion | flops 3645701376 | bytes 11799552 | tf_op jit(solution)/shard_map/dot_general | solution.py:86
  368.5 7.4 %convolution_convert_fusion.9 = bf16[768,768]{1,0:T(8,128)(2,1)} fusion(bf16[768,3072]{1,0:T(8,128)(2,1)} %copy-done.95, bf16[768,768]{1,0:T(8,128)(2,1)S(1)} %copy-done.57, bf16[768,768]{1,0:T(8,128)(2,1)S(1)} %copy-done.53, bf16[768,768]{1,0:T(8,128)(2,1)S(1)} %copy-done.46, bf16[768,768]{1,0:T(8,128)(2,1)S(1)} %copy-done.44), kind=kOutput, calls=%fused_computation.95 | convolution fusion | flops 3643342848 | bytes 10616832 | tf_op jit(solution)/shard_map/dot_general | solution.py:90
  377.0 17.1 %all-to-all-done.5 = bf16[8,96,768]{2,1,0:T(8,128)(2,1)S(1)} async-done(((bf16[8,96,768]{2,1,0:T(8,128)(2,1)}), bf16[8,96,768]{2,1,0:T(8,128)(2,1)S(1)}, u32[]{:S(2)}, u32[]{:S(2)}) %all-to-all-start.5) | async-done | bytes 1179680 | tf_op jit(solution)/shard_map/all_to_all | solution.py:209
  395.1 4.4 all-to-all-start.7
  421.8 6.1 all-to-all-done.7
  428.0 4.3 all-to-all-start.1
  453.3 7.0 %convert_reduce_fusion.1 = (f32[12,256,256]{1,2,0:T(8,128)}, bf16[2,12,256,256]{2,3,1,0:T(8,128)(2,1)S(1)}) fusion(f32[2,12,256,256]{2,3,1,0:T(8,128)} %get-tuple-element.101, f32[2,12,256]{2,1,0:T(8,128)S(1)} %get-tuple-element.100, f32[2,12,256,256]{2,3,1,0:T(8,128)S(1)} %bitcast.251, f32[2,12,256]{2,1,0:T(8,128)S(1)} %copy-done.72), kind=kLoop, calls=%fused_computation.22 | loop fusion | flops 8650752 | bytes 18923520 | tf_op jit(solution)/shard_map/reduce_sum | solution.py:271
  466.7 6.0 fusion.27
  472.7 6.3 all-to-all-start.3
  479.1 8.0 %fusion.71 = f32[32,12]{1,0:T(8,128)} fusion(f32[12,256,256]{1,2,0:T(8,128)} %get-tuple-element.58, s32[256,256]{0,1:T(8,128)} %copy-done.68), kind=kOutput, calls=%fused_computation.157 | convolution fusion | flops 304087040 | bytes 3409408 | tf_op jit(solution)/shard_map/hqk,qkb->bh/dot_general | solution.py:272
  498.1 8.7 %all-to-all-done.3 = bf16[8,96,768]{2,1,0:T(8,128)(2,1)S(1)} async-done(((bf16[8,96,768]{2,1,0:T(8,128)(2,1)}), bf16[8,96,768]{2,1,0:T(8,128)(2,1)S(1)}, u32[]{:S(2)}, u32[]{:S(2)}) %all-to-all-start.3) | async-done | bytes 1179680 | tf_op jit(solution)/shard_map/all_to_all | solution.py:209
  545.5 10.4 %collective-permute-done.37 = bf16[768,768]{1,0:T(8,128)(2,1)} collective-permute-done((bf16[768,768]{1,0:T(8,128)(2,1)}, bf16[768,768]{1,0:T(8,128)(2,1)}, u32[]{:S(2)}, u32[]{:S(2)}) %collective-permute-start.37) | collective-permute-done | bytes 1179680 | tf_op jit(solution)/shard_map/ppermute | solution.py:50
  557.9 20.6 %collective-permute-done.31 = bf16[768,768]{1,0:T(8,128)(2,1)S(1)} collective-permute-done((bf16[768,768]{1,0:T(8,128)(2,1)}, bf16[768,768]{1,0:T(8,128)(2,1)S(1)}, u32[]{:S(2)}, u32[]{:S(2)}) %collective-permute-start.31) | collective-permute-done | bytes 1179680 | tf_op jit(solution)/shard_map/ppermute | solution.py:50
  586.2 5.9 collective-permute-done.22
  597.8 5.1 collective-permute-start.24
  (453 shorter events, 290.2 us)
Async XLA Ops:
  7.2 126.1 %all-gather.2.cloned.1.call-start = ((), (), s32[]{:S(2)}) async-start(), calls=%async_computation.9 | async-start | bytes 5068800 | tf_op jit(solution)/shard_map/all_gather | solution.py:133
  9.6 67.0 %collective-permute-start = (bf16[2,768,768]{2,1,0:T(8,128)(2,1)}, bf16[2,768,768]{2,1,0:T(8,128)(2,1)}, u32[]{:S(2)}, u32[]{:S(2)}) collective-permute-start(bf16[2,768,768]{2,1,0:T(8,128)(2,1)} %param.20), channel_id=1, source_target_pairs={{0,16},{8,24},{16,0},{24,8},{1,17},{9,25},{17,1},{25,9},{2,18},{10... | collective-permute-start | bytes 7077896 | tf_op jit(solution)/shard_map/ppermute | solution.py:42
  12.7 163.3 %collective-permute-start.1 = (bf16[2,768,768]{2,1,0:T(8,128)(2,1)}, bf16[2,768,768]{2,1,0:T(8,128)(2,1)}, u32[]{:S(2)}, u32[]{:S(2)}) collective-permute-start(bf16[2,768,768]{2,1,0:T(8,128)(2,1)} %param.20), channel_id=1, source_target_pairs={{0,8},{8,0},{16,24},{24,16},{1,9},{9,1},{17,25},{25,17},{2,10},{10... | collective-permute-start | bytes 7077896 | tf_op jit(solution)/shard_map/ppermute | solution.py:42
  12.7 114.2 %collective-permute-start.3 = (bf16[2,768,768]{2,1,0:T(8,128)(2,1)}, bf16[2,768,768]{2,1,0:T(8,128)(2,1)}, u32[]{:S(2)}, u32[]{:S(2)}) collective-permute-start(bf16[2,768,768]{2,1,0:T(8,128)(2,1)} %param.21), channel_id=1, source_target_pairs={{0,16},{8,24},{16,0},{24,8},{1,17},{9,25},{17,1},{25,9},{2,18},{10... | collective-permute-start | bytes 7077896 | tf_op jit(solution)/shard_map/ppermute | solution.py:42
  12.8 166.3 %collective-permute-start.4 = (bf16[2,768,768]{2,1,0:T(8,128)(2,1)}, bf16[2,768,768]{2,1,0:T(8,128)(2,1)}, u32[]{:S(2)}, u32[]{:S(2)}) collective-permute-start(bf16[2,768,768]{2,1,0:T(8,128)(2,1)} %param.21), channel_id=1, source_target_pairs={{0,8},{8,0},{16,24},{24,16},{1,9},{9,1},{17,25},{25,17},{2,10},{10... | collective-permute-start | bytes 7077896 | tf_op jit(solution)/shard_map/ppermute | solution.py:42
  76.6 105.7 %collective-permute-start.2 = (bf16[2,768,768]{2,1,0:T(8,128)(2,1)}, bf16[2,768,768]{2,1,0:T(8,128)(2,1)}, u32[]{:S(2)}, u32[]{:S(2)}) collective-permute-start(bf16[2,768,768]{2,1,0:T(8,128)(2,1)} %collective-permute-done), channel_id=1, source_target_pairs={{0,8},{8,0},{16,24},{24,16},{1,9},{9,1},{17,25},{25,17},{2,10},{10... | collective-permute-start | bytes 7077896 | tf_op jit(solution)/shard_map/ppermute | solution.py:42
  126.9 82.7 %collective-permute-start.5 = (bf16[2,768,768]{2,1,0:T(8,128)(2,1)}, bf16[2,768,768]{2,1,0:T(8,128)(2,1)}, u32[]{:S(2)}, u32[]{:S(2)}) collective-permute-start(bf16[2,768,768]{2,1,0:T(8,128)(2,1)} %collective-permute-done.3), channel_id=1, source_target_pairs={{0,8},{8,0},{16,24},{24,16},{1,9},{9,1},{17,25},{25,17},{2,10},{10... | collective-permute-start | bytes 7077896 | tf_op jit(solution)/shard_map/ppermute | solution.py:42
  169.9 35.4 %all-to-all-start = ((bf16[8,96,768]{2,1,0:T(8,128)(2,1)}), bf16[8,96,768]{2,1,0:T(8,128)(2,1)}, u32[]{:S(2)}, u32[]{:S(2)}) async-start(bf16[8,96,768]{2,1,0:T(8,128)(2,1)} %bitcast.10), calls=%async_computation | async-start | bytes 2359296 | tf_op jit(solution)/shard_map/all_to_all | solution.py:209
  205.3 32.7 %all-to-all-start.4 = ((bf16[8,96,768]{2,1,0:T(8,128)(2,1)}), bf16[8,96,768]{2,1,0:T(8,128)(2,1)}, u32[]{:S(2)}, u32[]{:S(2)}) async-start(bf16[8,96,768]{2,1,0:T(8,128)(2,1)} %bitcast.281), calls=%async_computation.4 | async-start | bytes 2359296 | tf_op jit(solution)/shard_map/all_to_all | solution.py:209
  238.0 38.1 %all-to-all-start.2 = ((bf16[8,96,768]{2,1,0:T(8,128)(2,1)}), bf16[8,96,768]{2,1,0:T(8,128)(2,1)S(1)}, u32[]{:S(2)}, u32[]{:S(2)}) async-start(bf16[8,96,768]{2,1,0:T(8,128)(2,1)} %bitcast.22), calls=%async_computation.2 | async-start | bytes 2359296 | tf_op jit(solution)/shard_map/all_to_all | solution.py:209
  276.0 34.5 %all-to-all-start.6 = ((bf16[8,96,768]{2,1,0:T(8,128)(2,1)}), bf16[8,96,768]{2,1,0:T(8,128)(2,1)S(1)}, u32[]{:S(2)}, u32[]{:S(2)}) async-start(bf16[8,96,768]{2,1,0:T(8,128)(2,1)} %bitcast.280), calls=%async_computation.6 | async-start | bytes 2359296 | tf_op jit(solution)/shard_map/all_to_all | solution.py:209
  357.8 166.8 %collective-permute-start.32 = (bf16[768,768]{1,0:T(8,128)(2,1)}, bf16[768,768]{1,0:T(8,128)(2,1)}, u32[]{:S(2)}, u32[]{:S(2)}) collective-permute-start(bf16[768,768]{1,0:T(8,128)(2,1)} %convolution_convert_fusion.4), channel_id=1, source_target_pairs={{0,8},{8,0},{16,24},{24,16},{1,9},{9,1},{17,25},{25,17},{2,10},{10... | collective-permute-start | bytes 3538952 | tf_op jit(solution)/shard_map/ppermute | solution.py:50
  357.8 43.9 %collective-permute-start.33 = (bf16[768,768]{1,0:T(8,128)(2,1)}, bf16[768,768]{1,0:T(8,128)(2,1)}, u32[]{:S(2)}, u32[]{:S(2)}) collective-permute-start(bf16[768,768]{1,0:T(8,128)(2,1)} %convolution_convert_fusion.3), channel_id=1, source_target_pairs={{0,8},{8,0},{16,24},{24,16},{1,9},{9,1},{17,25},{25,17},{2,10},{10... | collective-permute-start | bytes 3538952 | tf_op jit(solution)/shard_map/ppermute | solution.py:50
  358.3 47.6 %collective-permute-start.27 = (bf16[768,768]{1,0:T(8,128)(2,1)}, bf16[768,768]{1,0:T(8,128)(2,1)}, u32[]{:S(2)}, u32[]{:S(2)}) collective-permute-start(bf16[768,768]{1,0:T(8,128)(2,1)} %convolution_convert_fusion.7), channel_id=1, source_target_pairs={{0,8},{8,0},{16,24},{24,16},{1,9},{9,1},{17,25},{25,17},{2,10},{10... | collective-permute-start | bytes 3538952 | tf_op jit(solution)/shard_map/ppermute | solution.py:50
  358.3 53.2 %collective-permute-start.36 = (bf16[768,768]{1,0:T(8,128)(2,1)}, bf16[768,768]{1,0:T(8,128)(2,1)}, u32[]{:S(2)}, u32[]{:S(2)}) collective-permute-start(bf16[768,768]{1,0:T(8,128)(2,1)} %convolution_convert_fusion.1), channel_id=1, source_target_pairs={{0,8},{8,0},{16,24},{24,16},{1,9},{9,1},{17,25},{25,17},{2,10},{10... | collective-permute-start | bytes 3538952 | tf_op jit(solution)/shard_map/ppermute | solution.py:50
  358.8 57.1 %collective-permute-start.30 = (bf16[768,768]{1,0:T(8,128)(2,1)}, bf16[768,768]{1,0:T(8,128)(2,1)}, u32[]{:S(2)}, u32[]{:S(2)}) collective-permute-start(bf16[768,768]{1,0:T(8,128)(2,1)} %convolution_convert_fusion.5), channel_id=1, source_target_pairs={{0,8},{8,0},{16,24},{24,16},{1,9},{9,1},{17,25},{25,17},{2,10},{10... | collective-permute-start | bytes 3538952 | tf_op jit(solution)/shard_map/ppermute | solution.py:50
  360.9 33.2 %all-to-all-start.5 = ((bf16[8,96,768]{2,1,0:T(8,128)(2,1)}), bf16[8,96,768]{2,1,0:T(8,128)(2,1)S(1)}, u32[]{:S(2)}, u32[]{:S(2)}) async-start(bf16[8,96,768]{2,1,0:T(8,128)(2,1)} %bitcast.38), calls=%async_computation.5 | async-start | bytes 2359296 | tf_op jit(solution)/shard_map/all_to_all | solution.py:209
  395.1 32.8 %all-to-all-start.7 = ((bf16[8,96,768]{2,1,0:T(8,128)(2,1)}), bf16[8,96,768]{2,1,0:T(8,128)(2,1)}, u32[]{:S(2)}, u32[]{:S(2)}) async-start(bf16[8,96,768]{2,1,0:T(8,128)(2,1)} %bitcast.42), calls=%async_computation.7 | async-start | bytes 2359296 | tf_op jit(solution)/shard_map/all_to_all | solution.py:209
  401.7 137.1 %collective-permute-start.26 = (bf16[768,768]{1,0:T(8,128)(2,1)}, bf16[768,768]{1,0:T(8,128)(2,1)}, u32[]{:S(2)}, u32[]{:S(2)}) collective-permute-start(bf16[768,768]{1,0:T(8,128)(2,1)} %convolution_convert_fusion.8), channel_id=1, source_target_pairs={{0,8},{8,0},{16,24},{24,16},{1,9},{9,1},{17,25},{25,17},{2,10},{10... | collective-permute-start | bytes 3538952 | tf_op jit(solution)/shard_map/ppermute | solution.py:50
  405.9 133.1 %collective-permute-start.34 = (bf16[768,768]{1,0:T(8,128)(2,1)}, bf16[768,768]{1,0:T(8,128)(2,1)}, u32[]{:S(2)}, u32[]{:S(2)}) collective-permute-start(bf16[768,768]{1,0:T(8,128)(2,1)} %add_convert_fusion.1), channel_id=1, source_target_pairs={{0,16},{8,24},{16,0},{24,8},{1,17},{9,25},{17,1},{25,9},{2,18},{10... | collective-permute-start | bytes 3538952 | tf_op jit(solution)/shard_map/ppermute | solution.py:50
  411.5 130.9 %collective-permute-start.28 = (bf16[768,768]{1,0:T(8,128)(2,1)}, bf16[768,768]{1,0:T(8,128)(2,1)}, u32[]{:S(2)}, u32[]{:S(2)}) collective-permute-start(bf16[768,768]{1,0:T(8,128)(2,1)} %add_convert_fusion.3), channel_id=1, source_target_pairs={{0,16},{8,24},{16,0},{24,8},{1,17},{9,25},{17,1},{25,9},{2,18},{10... | collective-permute-start | bytes 3538952 | tf_op jit(solution)/shard_map/ppermute | solution.py:50
  428.0 44.8 %all-to-all-start.1 = ((bf16[8,96,768]{2,1,0:T(8,128)(2,1)}), bf16[8,96,768]{2,1,0:T(8,128)(2,1)}, u32[]{:S(2)}, u32[]{:S(2)}) async-start(bf16[8,96,768]{2,1,0:T(8,128)(2,1)} %bitcast.268), calls=%async_computation.1 | async-start | bytes 2359296 | tf_op jit(solution)/shard_map/all_to_all | solution.py:209
  472.7 34.1 %all-to-all-start.3 = ((bf16[8,96,768]{2,1,0:T(8,128)(2,1)}), bf16[8,96,768]{2,1,0:T(8,128)(2,1)S(1)}, u32[]{:S(2)}, u32[]{:S(2)}) async-start(bf16[8,96,768]{2,1,0:T(8,128)(2,1)} %bitcast.32), calls=%async_computation.3 | async-start | bytes 2359296 | tf_op jit(solution)/shard_map/all_to_all | solution.py:209
  489.4 21.1 %collective-permute-start.6 = (f32[1920]{0:T(1024)}, f32[1920]{0:T(1024)}, u32[]{:S(2)}, u32[]{:S(2)}) collective-permute-start(f32[1920]{0:T(1024)} %pad_maximum_fusion.21), channel_id=1, source_target_pairs={{0,8},{8,0},{16,24},{24,16},{1,9},{9,1},{17,25},{25,17},{2,10},{10... | collective-permute-start | bytes 23048 | tf_op jit(solution)/shard_map/ppermute | solution.py:77
  524.6 20.1 %collective-permute-start.35 = (bf16[768,768]{1,0:T(8,128)(2,1)}, bf16[768,768]{1,0:T(8,128)(2,1)}, u32[]{:S(2)}, u32[]{:S(2)}) collective-permute-start(bf16[768,768]{1,0:T(8,128)(2,1)} %convolution_convert_fusion.2), channel_id=1, source_target_pairs={{0,8},{8,0},{16,24},{24,16},{1,9},{9,1},{17,25},{25,17},{2,10},{10... | collective-permute-start | bytes 3538952 | tf_op jit(solution)/shard_map/ppermute | solution.py:50
  526.7 29.2 %collective-permute-start.37 = (bf16[768,768]{1,0:T(8,128)(2,1)}, bf16[768,768]{1,0:T(8,128)(2,1)}, u32[]{:S(2)}, u32[]{:S(2)}) collective-permute-start(bf16[768,768]{1,0:T(8,128)(2,1)} %add_convert_fusion), channel_id=1, source_target_pairs={{0,16},{8,24},{16,0},{24,8},{1,17},{9,25},{17,1},{25,9},{2,18},{10... | collective-permute-start | bytes 3538952 | tf_op jit(solution)/shard_map/ppermute | solution.py:50
  538.9 19.0 %collective-permute-start.29 = (bf16[768,768]{1,0:T(8,128)(2,1)}, bf16[768,768]{1,0:T(8,128)(2,1)S(1)}, u32[]{:S(2)}, u32[]{:S(2)}) collective-permute-start(bf16[768,768]{1,0:T(8,128)(2,1)} %convolution_convert_fusion.6), channel_id=1, source_target_pairs={{0,8},{8,0},{16,24},{24,16},{1,9},{9,1},{17,25},{25,17},{2,10},{10... | collective-permute-start | bytes 3538952 | tf_op jit(solution)/shard_map/ppermute | solution.py:50
  539.0 39.5 %collective-permute-start.31 = (bf16[768,768]{1,0:T(8,128)(2,1)}, bf16[768,768]{1,0:T(8,128)(2,1)S(1)}, u32[]{:S(2)}, u32[]{:S(2)}) collective-permute-start(bf16[768,768]{1,0:T(8,128)(2,1)} %add_convert_fusion.2), channel_id=1, source_target_pairs={{0,16},{8,24},{16,0},{24,8},{1,17},{9,25},{17,1},{25,9},{2,18},{10... | collective-permute-start | bytes 3538952 | tf_op jit(solution)/shard_map/ppermute | solution.py:50
  542.5 41.4 %collective-permute-start.21 = (bf16[2,2,2,2,24,784]{5,4,3,2,1,0:T(8,128)(2,1)S(1)}, bf16[2,2,2,2,24,784]{5,4,3,2,1,0:T(8,128)(2,1)S(1)}, u32[]{:S(2)}, u32[]{:S(2)}) collective-permute-start(bf16[2,2,2,2,24,784]{5,4,3,2,1,0:T(8,128)(2,1)S(1)} %copy-done.75), channel_id=1, source_target_pairs={{0,8},{8,0},{16,24},{24,16},{1,9},{9,1},{17,25},{25,17},{2,10},{10... | collective-permute-start | bytes 1806344 | tf_op jit(solution)/shard_map/ppermute | solution.py:69
  544.8 41.1 %collective-permute-start.11 = (bf16[2,2,2,2,24,1152]{5,4,2,1,0,3:T(8,128)(2,1)S(1)}, bf16[2,2,2,2,24,1152]{5,4,2,1,0,3:T(8,128)(2,1)S(1)}, u32[]{:S(2)}, u32[]{:S(2)}) collective-permute-start(bf16[2,2,2,2,24,1152]{5,4,2,1,0,3:T(8,128)(2,1)S(1)} %copy-done.70), channel_id=1, source_target_pairs={{0,8},{8,0},{16,24},{24,16},{1,9},{9,1},{17,25},{25,17},{2,10},{10... | collective-permute-start | bytes 2654216 | tf_op jit(solution)/shard_map/ppermute | solution.py:69
  555.9 47.1 %collective-permute-start.16 = (bf16[2,2,2,2,24,1152]{5,4,2,1,3,0:T(8,128)(2,1)S(1)}, bf16[2,2,2,2,24,1152]{5,4,2,1,3,0:T(8,128)(2,1)S(1)}, u32[]{:S(2)}, u32[]{:S(2)}) collective-permute-start(bf16[2,2,2,2,24,1152]{5,4,2,1,3,0:T(8,128)(2,1)S(1)} %copy-done.69), channel_id=1, source_target_pairs={{0,8},{8,0},{16,24},{24,16},{1,9},{9,1},{17,25},{25,17},{2,10},{10... | collective-permute-start | bytes 2654216 | tf_op jit(solution)/shard_map/ppermute | solution.py:69
  594.7 17.5 %collective-permute-start.12 = (bf16[2,2,2,24,1152]{4,3,2,1,0:T(8,128)(2,1)}, bf16[2,2,2,24,1152]{4,3,2,1,0:T(8,128)(2,1)}, u32[]{:S(2)}, u32[]{:S(2)}) collective-permute-start(bf16[2,2,2,24,1152]{4,3,2,1,0:T(8,128)(2,1)} %fusion.104), channel_id=1, source_target_pairs={{0,1},{1,0},{2,3},{3,2},{4,5},{5,4},{6,7},{7,6},{8,9},{9,8},{10,11... | collective-permute-start | bytes 1327112 | tf_op jit(solution)/shard_map/ppermute | solution.py:69
  (118 other events, 841.1 us)
Sparse Core Ops, SparseCore 0:
  11.4 76.7 all-gather.1

commit v2 on v1

--- a/solution.py
+++ b/solution.py
@@ -36,20 +36,34 @@
     return [1 << i for i in range(size.bit_length() - 1)]
 
 
-def gather_relative(block, size):
+def gather_far(block, size):
     blocks = [block]
-    for bit in reversed(bits_of(size)):
+    for bit in reversed(bits_of(size)[1:]):
         blocks = blocks + [lax.ppermute(b, "dp", flip_pairs(size, bit)) for b in blocks]
     return blocks
 
 
-def scatter_relative(parts, size):
-    for bit in bits_of(size):
+def gather_near(blocks, size):
+    return blocks + [lax.ppermute(b, "dp", flip_pairs(size, 1)) for b in blocks]
+
+
+def scatter_near(parts, size):
+    half = len(parts) // 2
+    arrived = [
+        lax.ppermute(p.astype(jnp.bfloat16), "dp", flip_pairs(size, 1)) for p in parts[half:]
+    ]
+    return [p.astype(jnp.float32) + q.astype(jnp.float32) for p, q in zip(parts[:half], arrived)]
+
+
+def scatter_far(parts, size):
+    for bit in bits_of(size)[1:]:
         half = len(parts) // 2
         arrived = [
             lax.ppermute(p.astype(jnp.bfloat16), "dp", flip_pairs(size, bit)) for p in parts[half:]
         ]
-        parts = [p.astype(jnp.float32) + q.astype(jnp.float32) for p, q in zip(parts[:half], arrived)]
+        parts = [
+            p.astype(jnp.float32) + q.astype(jnp.float32) for p, q in zip(parts[:half], arrived)
+        ]
     return parts[0]
 
 
@@ -134,8 +148,11 @@
     qkv_full = packed_full[:, : 3 * model_width]
     out_full = packed_full[:, 3 * model_width : 4 * model_width]
     router_full = packed_full[:, 4 * model_width : 4 * model_width + experts]
-    in_blocks = gather_relative(expert_in, sizes["dp"])
-    back_blocks = gather_relative(expert_out, sizes["dp"])
+    far_blocks = [
+        gather_far(weight[e], sizes["dp"])
+        for e in range(local_experts)
+        for weight in (expert_in, expert_out)
+    ]
     flat_x = tokens.astype(jnp.float32).reshape(row_count, model_width)
     normed_low = rms_norm(flat_x, gain_attn).astype(jnp.bfloat16)
     qkv_act = jnp.dot(normed_low, qkv_full, preferred_element_type=jnp.float32).astype(jnp.bfloat16)
@@ -170,6 +187,9 @@
         preferred_element_type=jnp.float32,
     )
     context = context.reshape(row_count, model_width).astype(jnp.bfloat16)
+    far_blocks = lax.optimization_barrier((far_blocks, context))[0]
+    near_blocks = [gather_near(blocks, sizes["dp"]) for blocks in far_blocks]
+    in_blocks, back_blocks = near_blocks[0::2], near_blocks[1::2]
     middle = flat_x + jnp.dot(context, out_full, preferred_element_type=jnp.float32)
     ffn_low = rms_norm(middle, gain_ffn).astype(jnp.bfloat16)
     logits = jnp.dot(ffn_low, router_full, preferred_element_type=jnp.float32)
@@ -218,8 +238,8 @@
         )
     produced, grad_back, gate_terms, in_grads, out_grads = [], [], [], [], []
     for e in range(local_experts):
-        in_full = jnp.concatenate([b[e] for b in in_blocks], axis=1)
-        back_full = jnp.concatenate([b[e] for b in back_blocks], axis=0)
+        in_full = jnp.concatenate(in_blocks[e], axis=1)
+        back_full = jnp.concatenate(back_blocks[e], axis=0)
         block_width = expert_in.shape[2]
         pre_act = dot_nn(received[e], in_full)
         hidden = gelu_tanh(pre_act).astype(jnp.bfloat16)
@@ -233,13 +253,18 @@
         produced.append(made)
         cuts = [slice(r * block_width, (r + 1) * block_width) for r in range(sizes["dp"])]
         out_grads.append(
-            scatter_relative([dot_tn(hidden[:, c], grad_recv[e]) for c in cuts], sizes["dp"])
+            scatter_near([dot_tn(hidden[:, c], grad_recv[e]) for c in cuts], sizes["dp"])
         )
         in_grads.append(
-            scatter_relative([dot_tn(received[e], grad_pre[:, c]) for c in cuts], sizes["dp"])
+            scatter_near([dot_tn(received[e], grad_pre[:, c]) for c in cuts], sizes["dp"])
         )
-    expert_in_grad = jnp.stack(in_grads)
-    expert_out_grad = jnp.stack(out_grads)
+    out_grads, in_grads, grad_back = lax.optimization_barrier((
+        [[p[0]] + [q.astype(jnp.bfloat16) for q in p[1:]] for p in out_grads],
+        [[p[0]] + [q.astype(jnp.bfloat16) for q in p[1:]] for p in in_grads],
+        grad_back,
+    ))
+    out_grads = [scatter_far(parts, sizes["dp"]) for parts in out_grads]
+    in_grads = [scatter_far(parts, sizes["dp"]) for parts in in_grads]
     terms = jnp.stack([t.reshape(sizes["expert"], group_rows) for t in gate_terms], axis=1)
     terms = lax.all_to_all(terms, "expert", split_axis=0, concat_axis=0, tiled=True)
     terms = jnp.transpose(terms, (1, 0, 2)).reshape(1, local_experts * slot_rows)
@@ -292,6 +317,9 @@
         ],
         axis=1,
     ).astype(jnp.bfloat16)
+    out_grads, in_grads, grad_qkv = lax.optimization_barrier((out_grads, in_grads, grad_qkv))
+    expert_in_grad = jnp.stack(in_grads)
+    expert_out_grad = jnp.stack(out_grads)
     qkv_part = jnp.einsum("nc,nd->cd", normed_low, grad_qkv, preferred_element_type=jnp.float32)
     grad_normed = jnp.einsum("nd,cd->nc", grad_qkv, qkv_full, preferred_element_type=jnp.float32)
     grad_x_part, gain_attn_part = jax.vjp(rms_norm, flat_x, gain_attn)[1](grad_normed)

time: 656 us -> 604 us (0.921)
  waiting for transfers between devices: 214 us -> 152 us
  starting transfers between devices: 75.3 us -> 83.2 us
    ppermute x18 -> x24, waiting for transfers between devices: 112 us -> 11.4 us  [the longest x4 11.3 us: gather_far(): lax.ppermute(b, 'dp', flip_pairs(size, bit))]
    all_gather x1, waiting for transfers between devices: 0.01 us -> 42.3 us  [on_device(): packed_full = lax.all_gather(packed, ('dp', 'expert'), axis=0, tiled=True)]
    ppermute x15, waiting for transfers between devices: 24.9 us -> 59.3 us  [halving_scatter(): lax.ppermute(send.astype(jnp.bfloat16), axis, flip_pairs(sizes[axis], bit))]
    all_to_all x8, waiting for transfers between devices: 67.9 us -> 33.7 us  [exchange(): lax.all_to_all(sent, 'expert', split_axis=0, concat_axis=0, tiled=True)]
    unnamed x214 -> x170, local copies, waits for them, and re-layouts: 14.8 us -> 38 us
    squeeze x8 -> x2, local copies, waits for them, and re-layouts: 22.4 us -> 4.94 us  [on_device(): weight[e]]
    dot_general x5, matrix products: 42.8 us -> 34.3 us  [dot_nt(): lax.dot_general(a, b, (((1,), (1,)), ((), ())), preferred_element_type=jn...]
    concatenate x1 -> x4, local copies, waits for them, and re-layouts: 0.05 us -> 8.45 us  [the longest x2 4.75 us: on_device(): in_full = jnp.concatenate(in_blocks[e], axis=1)]
  transfers between devices with their start and end apart: 48 -> 54, of which waited for: 24 -> 20; matrix products, arithmetic and copies ran while one was open for 45% -> 47% of each run, Pallas kernels for 0% -> 0%
where the time goes in v2:
time: 604 us; the launch traced here: 598 us
  matrix products  206 us (34%)
  waiting for transfers between devices  152 us (25%)
  local copies, waits for them, and re-layouts  96.1 us (16%)
  starting transfers between devices  83.2 us (14%)
  other arithmetic  45.4 us (8%)
  between operations  15.7 us (3%)
    dot_general x21, matrix products, dot_tn(): lax.dot_general(a, b, (((0,), (0,)), ((), ())), preferred_element_type=jn...  72.5 us
    ppermute x15, waiting for transfers between devices, halving_scatter(): lax.ppermute(send.astype(jnp.bfloat16), axis, flip_pairs(sizes[axis], bit))  59.3 us
    dot_general x8, matrix products, dot_nn(): lax.dot_general(a, b, (((1,), (0,)), ((), ())), preferred_element_type=jn...  52.4 us
    all_gather x1, waiting for transfers between devices, on_device(): packed_full = lax.all_gather(packed, ('dp', 'expert'), axis=0, tiled=True)  42.3 us
    all_to_all x8, starting transfers between devices, exchange(): lax.all_to_all(sent, 'expert', split_axis=0, concat_axis=0, tiled=True)  40.5 us
    unnamed x170, local copies, waits for them, and re-layouts  38 us
    dot_general x5, matrix products, dot_nt(): lax.dot_general(a, b, (((1,), (1,)), ((), ())), preferred_element_type=jn...  34.3 us
    all_to_all x8, waiting for transfers between devices, exchange(): lax.all_to_all(sent, 'expert', split_axis=0, concat_axis=0, tiled=True)  33.7 us
  transfers between devices with their start and end apart: 54, of which 20 were waited for; matrix products, arithmetic and copies ran while one was open for 47% of the time, Pallas kernels for 0%

profile of v2, /device:TPU:0, one launch (start us, length us, event | category | flops | bytes accessed | tf_op | source)
XLA Modules:
  0.0 598.3 jit_solution(5038082005404533145)
XLA Ops:
  23.1 12.0 %copy.124 = pred[256,256,32]{1,2,0:T(32,128)(4,1)S(1)} copy(pred[256,256,32]{0,2,1:T(32,128)(4,1)S(1)} %iota_compare_fusion) | data formatting | bytes 4194304 | tf_op jit(solution)/shard_map/eq | solution.py:176
  46.0 42.3 %all-gather.2.cloned.1.call-done = bf16[768,3200]{1,0:T(8,128)(2,1)} async-done(((bf16[24,3200]{1,0:T(8,128)(2,1)}), bf16[768,3200]{1,0:T(8,128)(2,1)}) %all-gather.2.cloned.1.call-update) | async-done | bytes 4915216 | tf_op jit(solution)/shard_map/all_gather | solution.py:147
  104.6 5.7 fusion.149
  118.9 11.3 %collective-permute-done.1 = bf16[768,768]{1,0:T(8,128)(2,1)} collective-permute-done((bf16[768,768]{1,0:T(8,128)(2,1)}, bf16[768,768]{1,0:T(8,128)(2,1)}, u32[]{:S(2)}, u32[]{:S(2)}) %collective-permute-start.1) | collective-permute-done | bytes 1179680 | tf_op jit(solution)/shard_map/ppermute | solution.py:42
  138.7 6.4 %all-to-all-start.5 = ((bf16[8,96,768]{2,1,0:T(8,128)(2,1)}), bf16[8,96,768]{2,1,0:T(8,128)(2,1)}, u32[]{:S(2)}, u32[]{:S(2)}) async-start(bf16[8,96,768]{2,1,0:T(8,128)(2,1)} %bitcast.26), calls=%async_computation.5 | async-start | bytes 2359296 | tf_op jit(solution)/shard_map/all_to_all | solution.py:229
  166.1 8.3 %all-to-all-done.5 = bf16[8,96,768]{2,1,0:T(8,128)(2,1)} async-done(((bf16[8,96,768]{2,1,0:T(8,128)(2,1)}), bf16[8,96,768]{2,1,0:T(8,128)(2,1)}, u32[]{:S(2)}, u32[]{:S(2)}) %all-to-all-start.5) | async-done | bytes 1179680 | tf_op jit(solution)/shard_map/all_to_all | solution.py:229
  174.4 4.3 all-to-all-start.2
  201.1 7.7 %fusion.151 = f32[768,3072]{1,0:T(8,128)} fusion(bf16[768,768]{1,0:T(8,128)(2,1)} %bitcast.27, bf16[3072,768]{1,0:T(8,128)(2,1)S(1)} %constant_dynamic-update-slice_fusion.12), kind=kOutput, calls=%fused_computation.291 | convolution fusion | flops 3623878656 | bytes 15335424 | tf_op jit(solution)/shard_map/dot_general | solution.py:104
  208.7 6.2 %all-to-all-start.4 = ((bf16[8,96,768]{2,1,0:T(8,128)(2,1)}), bf16[8,96,768]{2,1,0:T(8,128)(2,1)}, u32[]{:S(2)}, u32[]{:S(2)}) async-start(bf16[8,96,768]{2,1,0:T(8,128)(2,1)} %bitcast.256), calls=%async_computation.4 | async-start | bytes 2359296 | tf_op jit(solution)/shard_map/all_to_all | solution.py:229
  215.0 12.7 %fusion.13 = (bf16[768,3072]{1,0:T(8,128)(2,1)S(1)}, bf16[768,3072]{1,0:T(8,128)(2,1)S(1)}) fusion(f32[768,3072]{1,0:T(8,128)} %fusion.151, bf16[768,768]{1,0:T(8,128)(2,1)} %bitcast.19, bf16[768,3072]{1,0:T(8,128)(2,1)} %constant_dynamic-update-slice_fusion.8), kind=kOutput, calls=%fused_computation.17 | convolution fusion | flops 3675783168 | bytes 24772608 | tf_op jit(solution)/shard_map/dot_general | solution.py:100
  227.7 4.3 convolution_convert_fusion.3
  243.1 4.7 all-to-all-start
  251.7 10.4 %fusion.150 = f32[768,3072]{1,0:T(8,128)} fusion(bf16[768,768]{1,0:T(8,128)(2,1)} %bitcast.25, bf16[3072,768]{1,0:T(8,128)(2,1)} %constant_dynamic-update-slice_fusion.4), kind=kOutput, calls=%fused_computation.290 | convolution fusion | flops 3623878656 | bytes 15335424 | tf_op jit(solution)/shard_map/dot_general | solution.py:104
  262.1 4.9 convolution_convert_fusion.1
  267.0 9.0 %all-to-all-done = bf16[8,96,768]{2,1,0:T(8,128)(2,1)} async-done(((bf16[8,96,768]{2,1,0:T(8,128)(2,1)}), bf16[8,96,768]{2,1,0:T(8,128)(2,1)}, u32[]{:S(2)}, u32[]{:S(2)}) %all-to-all-start) | async-done | bytes 1179680 | tf_op jit(solution)/shard_map/all_to_all | solution.py:229
  276.0 14.3 %fusion.6 = (bf16[768,3072]{1,0:T(8,128)(2,1)S(1)}, bf16[768,3072]{1,0:T(8,128)(2,1)}) fusion(f32[768,3072]{1,0:T(8,128)} %fusion.150, bf16[768,768]{1,0:T(8,128)(2,1)} %bitcast.11, bf16[768,3072]{1,0:T(8,128)(2,1)} %constant_dynamic-update-slice_fusion), kind=kOutput, calls=%fused_computation.10 | convolution fusion | flops 3675783168 | bytes 24772608 | tf_op jit(solution)/shard_map/dot_general | solution.py:100
  290.3 8.9 %convolution_convert_fusion.2 = bf16[768,768]{1,0:T(8,128)(2,1)} fusion(bf16[768,3072]{1,0:T(8,128)(2,1)S(1)} %get-tuple-element.108, bf16[768,3072]{1,0:T(8,128)(2,1)} %constant_dynamic-update-slice_fusion), kind=kOutput, calls=%fused_computation.89 | convolution fusion | flops 3624468480 | bytes 10616832 | tf_op jit(solution)/shard_map/dot_general | solution.py:104
  306.5 6.0 %multiply_reduce_fusion.1 = (f32[768]{0:T(1024)S(1)}, bf16[768,768]{1,0:T(8,128)(2,1)}) fusion(bf16[8,96,768]{2,1,0:T(8,128)(2,1)} %all-to-all-done.5, bf16[768,3072]{1,0:T(8,128)(2,1)S(1)} %bitcast.291, bf16[3072,768]{1,0:T(8,128)(2,1)S(1)} %bitcast.266), kind=kOutput, calls=%fused_computation.51 | convolution fusion | flops 3626827008 | bytes 11799552 | tf_op jit(solution)/shard_map/dot_general | solution.py:100
  312.6 8.9 %multiply_reduce_fusion.2 = (f32[768]{0:T(1024)S(1)}, bf16[768,768]{1,0:T(8,128)(2,1)}) fusion(bf16[8,96,768]{2,1,0:T(8,128)(2,1)} %all-to-all-done.4, bf16[768,3072]{1,0:T(8,128)(2,1)} %get-tuple-element.109, bf16[3072,768]{1,0:T(8,128)(2,1)} %constant_dynamic-update-slice_fusion.4), kind=kOutput, calls=%fused_computation.52 | convolution fusion | flops 3626827008 | bytes 11799552 | tf_op jit(solution)/shard_map/dot_general | solution.py:100
  332.1 4.5 all-to-all-start.7
  354.6 9.8 %all-to-all-done.7 = bf16[8,96,768]{2,1,0:T(8,128)(2,1)} async-done(((bf16[8,96,768]{2,1,0:T(8,128)(2,1)}), bf16[8,96,768]{2,1,0:T(8,128)(2,1)}, u32[]{:S(2)}, u32[]{:S(2)}) %all-to-all-start.7) | async-done | bytes 1179680 | tf_op jit(solution)/shard_map/all_to_all | solution.py:229
  376.3 4.5 convert_add_fusion.6
  380.8 4.5 convert_add_fusion.4
  385.3 4.6 convert_add_fusion.7
  396.5 4.7 all-to-all-start.1
  427.0 7.3 %multiply_reduce_fusion = (f32[2,12,256]{2,1,0:T(8,128)S(1)}, f32[2,12,256,256]{2,3,1,0:T(8,128)}) fusion(f32[2,12,256,256]{2,3,1,0:T(8,128)} %get-tuple-element.126, f32[2,12,256]{2,1,0:T(8,128)S(1)} %copy-done.37, bf16[2,256,12,64]{1,0,3,2:T(2,128)(2,1)S(1)} %copy-done.17, bf16[2,256,12,64]{1,0,3,2:T(2,128)(2,1)} %copy-done.18), kind=kOutput, calls=%fused_computation.24 | convolution fusion | flops 206039040 | bytes 14204928 | tf_op jit(solution)/shard_map/mqhd,mkhd->mhqk/dot_general | solution.py:291
  434.3 7.1 %convert_reduce_fusion.1 = (f32[12,256,256]{1,2,0:T(8,128)}, bf16[2,12,256,256]{2,3,1,0:T(8,128)(2,1)S(1)}) fusion(f32[2,12,256,256]{2,3,1,0:T(8,128)} %get-tuple-element.135, f32[2,12,256]{2,1,0:T(8,128)S(1)} %get-tuple-element.134, f32[2,12,256,256]{2,3,1,0:T(8,128)S(1)} %bitcast.231, f32[2,12,256]{2,1,0:T(8,128)S(1)} %copy-done.37), kind=kLoop, calls=%fused_computation.22 | loop fusion | flops 8650752 | bytes 18923520 | tf_op jit(solution)/shard_map/reduce_sum | solution.py:296
  445.0 6.1 %all-to-all-start.3 = ((bf16[8,96,768]{2,1,0:T(8,128)(2,1)}), bf16[8,96,768]{2,1,0:T(8,128)(2,1)}, u32[]{:S(2)}, u32[]{:S(2)}) async-start(bf16[8,96,768]{2,1,0:T(8,128)(2,1)} %bitcast.252), calls=%async_computation.3 | async-start | bytes 2359296 | tf_op jit(solution)/shard_map/all_to_all | solution.py:229
  460.1 14.3 %collective-permute-done.40 = bf16[2,2,2,24,784]{4,3,2,1,0:T(8,128)(2,1)S(1)} collective-permute-done((bf16[2,2,2,24,784]{4,3,2,1,0:T(8,128)(2,1)S(1)}, bf16[2,2,2,24,784]{4,3,2,1,0:T(8,128)(2,1)S(1)}, u32[]{:S(2)}, u32[]{:S(2)}) %collective-permute-start.40) | collective-permute-done | bytes 301088 | tf_op jit(solution)/shard_map/ppermute | solution.py:83
  479.4 28.4 %collective-permute-done.41 = bf16[2,2,24,784]{3,2,1,0:T(8,128)(2,1)S(1)} collective-permute-done((bf16[2,2,24,784]{3,2,1,0:T(8,128)(2,1)S(1)}, bf16[2,2,24,784]{3,2,1,0:T(8,128)(2,1)S(1)}, u32[]{:S(2)}, u32[]{:S(2)}) %collective-permute-start.41) | collective-permute-done | bytes 150560 | tf_op jit(solution)/shard_map/ppermute | solution.py:83
  517.2 5.3 fusion.79
  564.8 4.5 collective-permute-done.30
  (422 shorter events, 288.7 us)
Async XLA Ops:
  7.2 81.1 %all-gather.2.cloned.1.call-start = ((), (), s32[]{:S(2)}) async-start(), calls=%async_computation.9 | async-start | bytes 5068800 | tf_op jit(solution)/shard_map/all_gather | solution.py:147
  13.0 105.8 %collective-permute-start.2 = (bf16[768,768]{1,0:T(8,128)(2,1)}, bf16[768,768]{1,0:T(8,128)(2,1)}, u32[]{:S(2)}, u32[]{:S(2)}) collective-permute-start(bf16[768,768]{1,0:T(8,128)(2,1)} %get-tuple-element.37), channel_id=1, source_target_pairs={{0,16},{8,24},{16,0},{24,8},{1,17},{9,25},{17,1},{25,9},{2,18},{10... | collective-permute-start | bytes 3538952 | tf_op jit(solution)/shard_map/ppermute | solution.py:42
  16.0 102.9 %collective-permute-start = (bf16[768,768]{1,0:T(8,128)(2,1)}, bf16[768,768]{1,0:T(8,128)(2,1)}, u32[]{:S(2)}, u32[]{:S(2)}) collective-permute-start(bf16[768,768]{1,0:T(8,128)(2,1)} %get-tuple-element.33), channel_id=1, source_target_pairs={{0,16},{8,24},{16,0},{24,8},{1,17},{9,25},{17,1},{25,9},{2,18},{10... | collective-permute-start | bytes 3538952 | tf_op jit(solution)/shard_map/ppermute | solution.py:42
  17.6 101.2 %collective-permute-start.3 = (bf16[768,768]{1,0:T(8,128)(2,1)}, bf16[768,768]{1,0:T(8,128)(2,1)}, u32[]{:S(2)}, u32[]{:S(2)}) collective-permute-start(bf16[768,768]{1,0:T(8,128)(2,1)} %get-tuple-element.39), channel_id=1, source_target_pairs={{0,16},{8,24},{16,0},{24,8},{1,17},{9,25},{17,1},{25,9},{2,18},{10... | collective-permute-start | bytes 3538952 | tf_op jit(solution)/shard_map/ppermute | solution.py:42
  19.6 110.6 %collective-permute-start.1 = (bf16[768,768]{1,0:T(8,128)(2,1)}, bf16[768,768]{1,0:T(8,128)(2,1)}, u32[]{:S(2)}, u32[]{:S(2)}) collective-permute-start(bf16[768,768]{1,0:T(8,128)(2,1)} %get-tuple-element.35), channel_id=1, source_target_pairs={{0,16},{8,24},{16,0},{24,8},{1,17},{9,25},{17,1},{25,9},{2,18},{10... | collective-permute-start | bytes 3538952 | tf_op jit(solution)/shard_map/ppermute | solution.py:42
  130.2 27.1 %collective-permute-start.4 = (bf16[768,768]{1,0:T(8,128)(2,1)}, bf16[768,768]{1,0:T(8,128)(2,1)}, u32[]{:S(2)}, u32[]{:S(2)}) collective-permute-start(bf16[768,768]{1,0:T(8,128)(2,1)} %get-tuple-element.33), channel_id=1, source_target_pairs={{0,8},{8,0},{16,24},{24,16},{1,9},{9,1},{17,25},{25,17},{2,10},{10... | collective-permute-start | bytes 3538952 | tf_op jit(solution)/shard_map/ppermute | solution.py:47
  138.7 35.7 %all-to-all-start.5 = ((bf16[8,96,768]{2,1,0:T(8,128)(2,1)}), bf16[8,96,768]{2,1,0:T(8,128)(2,1)}, u32[]{:S(2)}, u32[]{:S(2)}) async-start(bf16[8,96,768]{2,1,0:T(8,128)(2,1)} %bitcast.26), calls=%async_computation.5 | async-start | bytes 2359296 | tf_op jit(solution)/shard_map/all_to_all | solution.py:229
  146.5 42.4 %collective-permute-start.7 = (bf16[768,768]{1,0:T(8,128)(2,1)}, bf16[768,768]{1,0:T(8,128)(2,1)}, u32[]{:S(2)}, u32[]{:S(2)}) collective-permute-start(bf16[768,768]{1,0:T(8,128)(2,1)} %collective-permute-done.1), channel_id=1, source_target_pairs={{0,8},{8,0},{16,24},{24,16},{1,9},{9,1},{17,25},{25,17},{2,10},{10... | collective-permute-start | bytes 3538952 | tf_op jit(solution)/shard_map/ppermute | solution.py:47
  146.7 44.6 %collective-permute-start.8 = (bf16[768,768]{1,0:T(8,128)(2,1)}, bf16[768,768]{1,0:T(8,128)(2,1)}, u32[]{:S(2)}, u32[]{:S(2)}) collective-permute-start(bf16[768,768]{1,0:T(8,128)(2,1)} %get-tuple-element.37), channel_id=1, source_target_pairs={{0,8},{8,0},{16,24},{24,16},{1,9},{9,1},{17,25},{25,17},{2,10},{10... | collective-permute-start | bytes 3538952 | tf_op jit(solution)/shard_map/ppermute | solution.py:47
  157.3 36.5 %collective-permute-start.9 = (bf16[768,768]{1,0:T(8,128)(2,1)}, bf16[768,768]{1,0:T(8,128)(2,1)}, u32[]{:S(2)}, u32[]{:S(2)}) collective-permute-start(bf16[768,768]{1,0:T(8,128)(2,1)} %collective-permute-done.2), channel_id=1, source_target_pairs={{0,8},{8,0},{16,24},{24,16},{1,9},{9,1},{17,25},{25,17},{2,10},{10... | collective-permute-start | bytes 3538952 | tf_op jit(solution)/shard_map/ppermute | solution.py:47
  160.7 35.5 %collective-permute-start.10 = (bf16[768,768]{1,0:T(8,128)(2,1)}, bf16[768,768]{1,0:T(8,128)(2,1)}, u32[]{:S(2)}, u32[]{:S(2)}) collective-permute-start(bf16[768,768]{1,0:T(8,128)(2,1)} %get-tuple-element.39), channel_id=1, source_target_pairs={{0,8},{8,0},{16,24},{24,16},{1,9},{9,1},{17,25},{25,17},{2,10},{10... | collective-permute-start | bytes 3538952 | tf_op jit(solution)/shard_map/ppermute | solution.py:47
  163.5 34.1 %collective-permute-start.11 = (bf16[768,768]{1,0:T(8,128)(2,1)}, bf16[768,768]{1,0:T(8,128)(2,1)}, u32[]{:S(2)}, u32[]{:S(2)}) collective-permute-start(bf16[768,768]{1,0:T(8,128)(2,1)} %collective-permute-done.3), channel_id=1, source_target_pairs={{0,8},{8,0},{16,24},{24,16},{1,9},{9,1},{17,25},{25,17},{2,10},{10... | collective-permute-start | bytes 3538952 | tf_op jit(solution)/shard_map/ppermute | solution.py:47
  174.4 34.3 %all-to-all-start.2 = ((bf16[8,96,768]{2,1,0:T(8,128)(2,1)}), bf16[8,96,768]{2,1,0:T(8,128)(2,1)}, u32[]{:S(2)}, u32[]{:S(2)}) async-start(bf16[8,96,768]{2,1,0:T(8,128)(2,1)} %bitcast.258), calls=%async_computation.2 | async-start | bytes 2359296 | tf_op jit(solution)/shard_map/all_to_all | solution.py:229
  208.7 34.3 %all-to-all-start.4 = ((bf16[8,96,768]{2,1,0:T(8,128)(2,1)}), bf16[8,96,768]{2,1,0:T(8,128)(2,1)}, u32[]{:S(2)}, u32[]{:S(2)}) async-start(bf16[8,96,768]{2,1,0:T(8,128)(2,1)} %bitcast.256), calls=%async_computation.4 | async-start | bytes 2359296 | tf_op jit(solution)/shard_map/all_to_all | solution.py:229
  243.1 32.9 %all-to-all-start = ((bf16[8,96,768]{2,1,0:T(8,128)(2,1)}), bf16[8,96,768]{2,1,0:T(8,128)(2,1)}, u32[]{:S(2)}, u32[]{:S(2)}) async-start(bf16[8,96,768]{2,1,0:T(8,128)(2,1)} %bitcast.255), calls=%async_computation | async-start | bytes 2359296 | tf_op jit(solution)/shard_map/all_to_all | solution.py:229
  332.1 32.3 %all-to-all-start.7 = ((bf16[8,96,768]{2,1,0:T(8,128)(2,1)}), bf16[8,96,768]{2,1,0:T(8,128)(2,1)}, u32[]{:S(2)}, u32[]{:S(2)}) async-start(bf16[8,96,768]{2,1,0:T(8,128)(2,1)} %bitcast.257), calls=%async_computation.7 | async-start | bytes 2359296 | tf_op jit(solution)/shard_map/all_to_all | solution.py:229
  340.4 35.9 %collective-permute-start.14 = (bf16[768,768]{1,0:T(8,128)(2,1)}, bf16[768,768]{1,0:T(8,128)(2,1)}, u32[]{:S(2)}, u32[]{:S(2)}) collective-permute-start(bf16[768,768]{1,0:T(8,128)(2,1)} %convolution_convert_fusion.8), channel_id=1, source_target_pairs={{0,8},{8,0},{16,24},{24,16},{1,9},{9,1},{17,25},{25,17},{2,10},{10... | collective-permute-start | bytes 3538952 | tf_op jit(solution)/shard_map/ppermute | solution.py:53
  340.9 27.0 %collective-permute-start.13 = (bf16[768,768]{1,0:T(8,128)(2,1)}, bf16[768,768]{1,0:T(8,128)(2,1)}, u32[]{:S(2)}, u32[]{:S(2)}) collective-permute-start(bf16[768,768]{1,0:T(8,128)(2,1)} %convolution_convert_fusion.10), channel_id=1, source_target_pairs={{0,8},{8,0},{16,24},{24,16},{1,9},{9,1},{17,25},{25,17},{2,10},{10... | collective-permute-start | bytes 3538952 | tf_op jit(solution)/shard_map/ppermute | solution.py:53
  341.4 30.7 %collective-permute-start.17 = (bf16[768,768]{1,0:T(8,128)(2,1)}, bf16[768,768]{1,0:T(8,128)(2,1)}, u32[]{:S(2)}, u32[]{:S(2)}) collective-permute-start(bf16[768,768]{1,0:T(8,128)(2,1)} %convolution_convert_fusion.5), channel_id=1, source_target_pairs={{0,8},{8,0},{16,24},{24,16},{1,9},{9,1},{17,25},{25,17},{2,10},{10... | collective-permute-start | bytes 3538952 | tf_op jit(solution)/shard_map/ppermute | solution.py:53
  345.8 35.0 %collective-permute-start.18 = (bf16[768,768]{1,0:T(8,128)(2,1)}, bf16[768,768]{1,0:T(8,128)(2,1)}, u32[]{:S(2)}, u32[]{:S(2)}) collective-permute-start(bf16[768,768]{1,0:T(8,128)(2,1)} %convolution_convert_fusion.4), channel_id=1, source_target_pairs={{0,8},{8,0},{16,24},{24,16},{1,9},{9,1},{17,25},{25,17},{2,10},{10... | collective-permute-start | bytes 3538952 | tf_op jit(solution)/shard_map/ppermute | solution.py:53
  350.5 34.9 %collective-permute-start.12 = (bf16[768,768]{1,0:T(8,128)(2,1)}, bf16[768,768]{1,0:T(8,128)(2,1)}, u32[]{:S(2)}, u32[]{:S(2)}) collective-permute-start(bf16[768,768]{1,0:T(8,128)(2,1)} %convolution_convert_fusion.11), channel_id=1, source_target_pairs={{0,8},{8,0},{16,24},{24,16},{1,9},{9,1},{17,25},{25,17},{2,10},{10... | collective-permute-start | bytes 3538952 | tf_op jit(solution)/shard_map/ppermute | solution.py:53
  364.4 32.2 %all-to-all-start.6 = ((bf16[8,96,768]{2,1,0:T(8,128)(2,1)}), bf16[8,96,768]{2,1,0:T(8,128)(2,1)S(1)}, u32[]{:S(2)}, u32[]{:S(2)}) async-start(bf16[8,96,768]{2,1,0:T(8,128)(2,1)} %bitcast.254), calls=%async_computation.6 | async-start | bytes 2359296 | tf_op jit(solution)/shard_map/all_to_all | solution.py:229
  367.9 22.0 %collective-permute-start.16 = (bf16[768,768]{1,0:T(8,128)(2,1)}, bf16[768,768]{1,0:T(8,128)(2,1)S(1)}, u32[]{:S(2)}, u32[]{:S(2)}) collective-permute-start(bf16[768,768]{1,0:T(8,128)(2,1)} %convolution_convert_fusion.6), channel_id=1, source_target_pairs={{0,8},{8,0},{16,24},{24,16},{1,9},{9,1},{17,25},{25,17},{2,10},{10... | collective-permute-start | bytes 3538952 | tf_op jit(solution)/shard_map/ppermute | solution.py:53
  396.5 48.4 %all-to-all-start.1 = ((bf16[8,96,768]{2,1,0:T(8,128)(2,1)}), bf16[8,96,768]{2,1,0:T(8,128)(2,1)}, u32[]{:S(2)}, u32[]{:S(2)}) async-start(bf16[8,96,768]{2,1,0:T(8,128)(2,1)} %bitcast.253), calls=%async_computation.1 | async-start | bytes 2359296 | tf_op jit(solution)/shard_map/all_to_all | solution.py:229
  401.3 122.8 %collective-permute-start.20 = (bf16[768,768]{1,0:T(8,128)(2,1)}, bf16[768,768]{1,0:T(8,128)(2,1)}, u32[]{:S(2)}, u32[]{:S(2)}) collective-permute-start(bf16[768,768]{1,0:T(8,128)(2,1)} %add_convert_fusion.3), channel_id=1, source_target_pairs={{0,16},{8,24},{16,0},{24,8},{1,17},{9,25},{17,1},{25,9},{2,18},{10... | collective-permute-start | bytes 3538952 | tf_op jit(solution)/shard_map/ppermute | solution.py:62
  402.9 122.9 %collective-permute-start.21 = (bf16[768,768]{1,0:T(8,128)(2,1)}, bf16[768,768]{1,0:T(8,128)(2,1)}, u32[]{:S(2)}, u32[]{:S(2)}) collective-permute-start(bf16[768,768]{1,0:T(8,128)(2,1)} %add_convert_fusion.2), channel_id=1, source_target_pairs={{0,16},{8,24},{16,0},{24,8},{1,17},{9,25},{17,1},{25,9},{2,18},{10... | collective-permute-start | bytes 3538952 | tf_op jit(solution)/shard_map/ppermute | solution.py:62
  403.4 124.3 %collective-permute-start.22 = (bf16[768,768]{1,0:T(8,128)(2,1)}, bf16[768,768]{1,0:T(8,128)(2,1)}, u32[]{:S(2)}, u32[]{:S(2)}) collective-permute-start(bf16[768,768]{1,0:T(8,128)(2,1)} %add_convert_fusion.1), channel_id=1, source_target_pairs={{0,16},{8,24},{16,0},{24,8},{1,17},{9,25},{17,1},{25,9},{2,18},{10... | collective-permute-start | bytes 3538952 | tf_op jit(solution)/shard_map/ppermute | solution.py:62
  404.9 124.6 %collective-permute-start.23 = (bf16[768,768]{1,0:T(8,128)(2,1)}, bf16[768,768]{1,0:T(8,128)(2,1)}, u32[]{:S(2)}, u32[]{:S(2)}) collective-permute-start(bf16[768,768]{1,0:T(8,128)(2,1)} %add_convert_fusion), channel_id=1, source_target_pairs={{0,16},{8,24},{16,0},{24,8},{1,17},{9,25},{17,1},{25,9},{2,18},{10... | collective-permute-start | bytes 3538952 | tf_op jit(solution)/shard_map/ppermute | solution.py:62
  427.0 27.3 %collective-permute-start.39 = (bf16[2,2,2,2,24,784]{5,4,3,2,1,0:T(8,128)(2,1)}, bf16[2,2,2,2,24,784]{5,4,3,2,1,0:T(8,128)(2,1)}, u32[]{:S(2)}, u32[]{:S(2)}) collective-permute-start(bf16[2,2,2,2,24,784]{5,4,3,2,1,0:T(8,128)(2,1)} %fusion.105), channel_id=1, source_target_pairs={{0,8},{8,0},{16,24},{24,16},{1,9},{9,1},{17,25},{25,17},{2,10},{10... | collective-permute-start | bytes 1806344 | tf_op jit(solution)/shard_map/ppermute | solution.py:83
  445.0 66.2 %all-to-all-start.3 = ((bf16[8,96,768]{2,1,0:T(8,128)(2,1)}), bf16[8,96,768]{2,1,0:T(8,128)(2,1)}, u32[]{:S(2)}, u32[]{:S(2)}) async-start(bf16[8,96,768]{2,1,0:T(8,128)(2,1)} %bitcast.252), calls=%async_computation.3 | async-start | bytes 2359296 | tf_op jit(solution)/shard_map/all_to_all | solution.py:229
  474.5 33.4 %collective-permute-start.41 = (bf16[2,2,24,784]{3,2,1,0:T(8,128)(2,1)S(1)}, bf16[2,2,24,784]{3,2,1,0:T(8,128)(2,1)S(1)}, u32[]{:S(2)}, u32[]{:S(2)}) collective-permute-start(bf16[2,2,24,784]{3,2,1,0:T(8,128)(2,1)S(1)} %fusion.121), channel_id=1, source_target_pairs={{0,16},{8,24},{16,0},{24,8},{1,17},{9,25},{17,1},{25,9},{2,18},{10... | collective-permute-start | bytes 451592 | tf_op jit(solution)/shard_map/ppermute | solution.py:83
  541.0 20.8 %collective-permute-start.34 = (bf16[2,2,2,2,24,1152]{5,4,2,1,3,0:T(8,128)(2,1)}, bf16[2,2,2,2,24,1152]{5,4,2,1,3,0:T(8,128)(2,1)}, u32[]{:S(2)}, u32[]{:S(2)}) collective-permute-start(bf16[2,2,2,2,24,1152]{5,4,2,1,3,0:T(8,128)(2,1)} %fusion.88), channel_id=1, source_target_pairs={{0,8},{8,0},{16,24},{24,16},{1,9},{9,1},{17,25},{25,17},{2,10},{10... | collective-permute-start | bytes 2654216 | tf_op jit(solution)/shard_map/ppermute | solution.py:83
  (98 other events, 935.3 us)
Sparse Core Ops, SparseCore 0:
  11.4 76.7 all-gather.1
